TPU v7x, 256 devices: a whole 4x4x8 slice. The times are simulated.
256 devices in a mesh: tomo: 8 (over z), tilt: 32 (over y, x, core).
Axes of the slice: x: 4, y: 4, z: 8, core: 2. Of those that a mesh axis runs over, the one named last changes fastest.
Arguments:
- tilt_images: bfloat16 [8, 32, 1024, 1024], P('tomo', 'tilt'), may hold values from -6 to 6
- anchors: int32 [8, 32, 32, 2], P('tomo', 'tilt'), may hold values from 0 to 960
- euler: float32 [8, 3, 32], P('tomo'), may hold values from -3.140625 to 3.140625
- tilt_angle: float32 [8, 32], P('tomo', 'tilt'), may hold values from -1.05 to 1.05
- defocus: float32 [8, 32], P('tomo', 'tilt'), may hold values from 1 to 3
- warp: float32 [8, 32, 6], P('tomo', 'tilt'), may hold values from -0.1 to 0.1
- centers: float32 [3, 2048], replicated, may hold values from -20 to 20
- amplitudes: float32 [2048], replicated, may hold values from 0.01 to 0.05
- widths: float32 [2048], replicated, may hold values from 1 to 2.5
Outputs:
- template_grad: float32 [5, 2048], replicated
- warp_grad: float32 [8, 32, 6], P('tomo', 'tilt')
Inputs may be any that keep to these rules, and one draw needn't show every extreme that they name: `anchors`: every patch of 64 x 64 pixels lies inside its tilt image.
All inputs are finite; a program needn't handle non-finite values.
Results may differ from a plain program's by a relative error of at most 0.0005.
Values may be sent and summed in bfloat16 or wider, within the bound.
No kernel may reach another device: no remote copies, remote signals or barrier semaphores. Data moves between devices by JAX's collectives and lax.ppermute only.
A program may use at most 64 MiB of HBM per device.

v0:
```python
import math

import jax
import jax.numpy as jnp
from jax import lax
from jax.sharding import PartitionSpec as P

BOX = 64


PRECISE = lax.Precision.HIGHEST


def signed_freqs(size_box):
    positions = jnp.arange(size_box, dtype=jnp.int32)
    return jnp.where(positions < size_box // 2, positions, positions - size_box).astype(jnp.float32)


def about_z(rotation_angle):
    c, s = (jnp.cos(rotation_angle), jnp.sin(rotation_angle))
    nought = jnp.zeros_like(rotation_angle)
    unity = jnp.ones_like(rotation_angle)
    return jnp.stack(
        [
            jnp.stack([c, -s, nought], -1),
            jnp.stack([s, c, nought], -1),
            jnp.stack([nought, nought, unity], -1),
        ],
        -2,
    )


def about_y(rotation_angle):
    c, s = (jnp.cos(rotation_angle), jnp.sin(rotation_angle))
    nought = jnp.zeros_like(rotation_angle)
    unity = jnp.ones_like(rotation_angle)
    return jnp.stack(
        [
            jnp.stack([c, nought, s], -1),
            jnp.stack([nought, unity, nought], -1),
            jnp.stack([-s, nought, c], -1),
        ],
        -2,
    )


def rotations(euler_rows, tilt_list):
    rotation = jnp.einsum(
        "nab,nbc,ncd,nde->nae",
        about_y(tilt_list),
        about_z(euler_rows[0]),
        about_y(euler_rows[1]),
        about_z(euler_rows[2]),
        precision=PRECISE,
    )
    return rotation[:, :2, :]


def ctf_table(focus_list, frequency):
    radius = frequency[:, None] ** 2 + frequency[None, :] ** 2
    return -jnp.sin(focus_list[:, None, None] * radius[None] / frequency.shape[0] + 0.1)


def dft_rows(size_box):
    positions = jnp.arange(size_box, dtype=jnp.int32)
    product = positions[:, None] * positions[None, :] % size_box
    turned = 2.0 * math.pi * product.astype(jnp.float32) / size_box
    return jnp.concatenate([jnp.cos(turned), -jnp.sin(turned)], 0)


def transform(patches, dft_table):
    edge = patches.shape[-1]
    half_done = jnp.einsum("qx,pxy->pqy", dft_table, patches.astype(jnp.float32), precision=PRECISE)
    transformed = jnp.einsum("pqy,ry->pqr", half_done, dft_table, precision=PRECISE)
    real_part = transformed[:, :edge, :edge] - transformed[:, edge:, edge:]
    imag_part = transformed[:, :edge, edge:] + transformed[:, edge:, :edge]
    return jnp.concatenate([real_part, imag_part], -1) / edge


def slice_terms(
    spectrum,
    weight,
    projection,
    transfer,
    warp_row,
    centers,
    amplitudes,
    widths,
    frequency,
    loss_scale,
):
    edge = frequency.shape[0]
    phase_unit = 2.0 * math.pi / edge
    blur_unit = 2.0 * math.pi**2 / edge**2
    planar = jnp.dot(projection, centers, precision=PRECISE)
    affine = jnp.eye(2, dtype=jnp.float32) + warp_row[:4].reshape(2, 2)
    placed = jnp.dot(affine, planar, precision=PRECISE) + 20.0 * warp_row[4:6][:, None] + edge / 2
    freq_col = frequency[:, None]
    envelope = jnp.exp(-blur_unit * widths[None, :] ** 2 * freq_col**2)
    phase_x = phase_unit * freq_col * placed[0][None, :]
    phase_y = phase_unit * freq_col * placed[1][None, :]
    slice_xr = envelope * jnp.cos(phase_x)
    slice_xi = -envelope * jnp.sin(phase_x)
    slice_yr = amplitudes[None, :] * envelope * jnp.cos(phase_y)
    slice_yi = -amplitudes[None, :] * envelope * jnp.sin(phase_y)
    stack_x = jnp.concatenate([slice_xr, slice_xi], 0).astype(jnp.bfloat16)
    stack_y = jnp.concatenate([slice_yr, slice_yi], 0).astype(jnp.bfloat16)
    blocks = jnp.dot(stack_x, stack_y.T, preferred_element_type=jnp.float32)
    model_re = blocks[:edge, :edge] - blocks[edge:, edge:]
    model_im = blocks[:edge, edge:] + blocks[edge:, :edge]
    factor = -2.0 * loss_scale * weight * transfer
    grad_re = (factor * (spectrum[:, :edge] - transfer * model_re)).astype(jnp.bfloat16)
    grad_im = (factor * (spectrum[:, edge:] - transfer * model_im)).astype(jnp.bfloat16)
    grad_stack = jnp.concatenate(
        [jnp.concatenate([grad_re, grad_im], 1), jnp.concatenate([grad_im, -grad_re], 1)], 0
    )
    back_x = jnp.dot(grad_stack, stack_y, preferred_element_type=jnp.float32)
    back_y = jnp.dot(grad_stack.T, stack_x, preferred_element_type=jnp.float32)
    back_xr, back_xi = (back_x[:edge], back_x[edge:])
    back_yr, back_yi = (back_y[:edge], back_y[edge:])
    move_x = phase_unit * jnp.sum(freq_col * (slice_xi * back_xr - slice_xr * back_xi), 0)
    move_y = phase_unit * jnp.sum(freq_col * (slice_yi * back_yr - slice_yr * back_yi), 0)
    inner_x = slice_xr * back_xr + slice_xi * back_xi
    inner_y = slice_yr * back_yr + slice_yi * back_yi
    curve_sum = jnp.sum(freq_col**2 * (inner_x + inner_y), 0)
    grad_amp = jnp.sum(inner_y, 0) / amplitudes
    grad_width = -2.0 * blur_unit * widths * curve_sum
    moves = jnp.stack([move_x, move_y])
    grad_planar = jnp.dot(affine.T, moves, precision=PRECISE)
    grad_pos = jnp.dot(projection.T, grad_planar, precision=PRECISE)
    template = jnp.concatenate([grad_pos, grad_amp[None], grad_width[None]], 0)
    warp_part = jnp.stack(
        [
            jnp.sum(move_x * planar[0]),
            jnp.sum(move_x * planar[1]),
            jnp.sum(move_y * planar[0]),
            jnp.sum(move_y * planar[1]),
            20.0 * jnp.sum(move_x),
            20.0 * jnp.sum(move_y),
        ]
    )
    return (template, warp_part)


def run_patches(
    spectra,
    weights,
    projections,
    transfers,
    warp_rows,
    centers,
    amplitudes,
    widths,
    frequency,
    loss_scale,
):
    patch_count = spectra.shape[0]
    block_count = patch_count // 4

    def regroup(array):
        return array.reshape((block_count, 4) + array.shape[1:])

    stacked = (
        regroup(spectra),
        regroup(weights),
        regroup(projections),
        regroup(transfers),
        regroup(warp_rows),
    )

    def block_step(running, pieces):
        template, warp_part = jax.vmap(
            lambda d, w, p, c, r: slice_terms(
                d, w, p, c, r, centers, amplitudes, widths, frequency, loss_scale
            )
        )(*pieces)
        return (running + jnp.sum(template, 0), warp_part)

    running, warp_terms = lax.scan(
        block_step, jnp.zeros((5, centers.shape[1]), jnp.float32), stacked
    )
    return (running, warp_terms.reshape(patch_count, 6))


def owner_work(
    received,
    angles_all,
    focus_all,
    warp_all,
    euler,
    tilt_count,
    centers,
    amplitudes,
    widths,
    frequency,
    loss_scale,
):
    owned_count = received.shape[0]
    first_slot = lax.axis_index("tilt") * owned_count
    owned_euler = lax.dynamic_slice_in_dim(euler[0], first_slot, owned_count, 1)
    power_mean = jnp.sum(received[..., :BOX] ** 2 + received[..., BOX:] ** 2, 1) / tilt_count
    weight = 1.0 / (0.25 + power_mean)
    projections = rotations(
        jnp.repeat(owned_euler, tilt_count, axis=1), jnp.tile(angles_all[0], owned_count)
    )
    transfers = ctf_table(jnp.tile(focus_all[0], owned_count), frequency)
    warp_rows = jnp.tile(warp_all[0], (owned_count, 1))
    template, warp_terms = run_patches(
        received.reshape(owned_count * tilt_count, BOX, 2 * BOX),
        jnp.repeat(weight, tilt_count, axis=0),
        projections,
        transfers,
        warp_rows,
        centers,
        amplitudes,
        widths,
        frequency,
        loss_scale,
    )
    per_tilt = jnp.sum(warp_terms.reshape(owned_count, tilt_count, 6), 0)
    return (template, per_tilt)


def on_device(tilt_images, anchors, euler, tilt_angle, defocus, warp, centers, amplitudes, widths):
    images = tilt_images[0, 0]
    corners = anchors[0, 0]
    particle_count = corners.shape[0]
    tilt_count = lax.axis_size("tilt")
    frequency = signed_freqs(BOX)
    loss_scale = 1.0 / (particle_count * tilt_count)
    patches = jax.vmap(
        lambda corner: lax.dynamic_slice(images, (corner[0], corner[1]), (BOX, BOX))
    )(corners)
    spectra = transform(patches, dft_rows(BOX))
    received = lax.all_to_all(spectra[:, None], "tilt", split_axis=0, concat_axis=1, tiled=True)
    angles_all, focus_all, warp_all = (
        lax.all_gather(tilt_angle, "tilt", axis=1, tiled=True),
        lax.all_gather(defocus, "tilt", axis=1, tiled=True),
        lax.all_gather(warp, "tilt", axis=1, tiled=True),
    )
    template, per_tilt = owner_work(
        received,
        angles_all,
        focus_all,
        warp_all,
        euler,
        tilt_count,
        centers,
        amplitudes,
        widths,
        frequency,
        loss_scale,
    )
    warp_local = lax.psum_scatter(per_tilt, "tilt", scatter_dimension=0, tiled=True)
    template = lax.psum(template, ("tomo", "tilt"))
    return (template, warp_local.reshape(1, 1, 6))


def solution(mesh):
    placed = (
        P("tomo", "tilt", None, None),
        P("tomo", "tilt", None, None),
        P("tomo", None, None),
        P("tomo", "tilt"),
        P("tomo", "tilt"),
        P("tomo", "tilt", None),
        P(),
        P(),
        P(),
    )
    return jax.shard_map(
        on_device,
        mesh=mesh,
        in_specs=placed,
        out_specs=(P(), P("tomo", "tilt", None)),
        check_vma=False,
    )
```

profile of v0, /device:TPU:1, one launch (start us, length us, event | category | flops | bytes accessed | tf_op | source)
XLA Modules:
  0.0 716.6 jit_solution(7772000622493595437)
XLA Ops:
  1.6 92.4 %while.16 = (s32[]{:T(128)}, bf16[1024,1024]{1,0:T(8,128)(2,1)}, s32[32,2]{0,1:T(2,128)S(1)}, bf16[32,64,64]{2,1,0:T(8,128)(2,1)S(1)}, s32[]{:T(128)}) while((s32[]{:T(128)}, bf16[1024,1024]{1,0:T(8,128)(2,1)}, s32[32,2]{0,1:T(2,128)S(1)}, bf16[32,64,64]{2,1,0:T(8,128)(2,1)S(1)}, s32[]{:T(128)}) %tuple.118), condition=%wide.while_cond, body=%wide.while_body.sunk | while | flops 2 | bytes 24685 | solution.py:232
  2.2 2.2 bitcast_dynamic-update-slice_fusion.6
  5.1 2.2 bitcast_dynamic-update-slice_fusion.6
  8.0 2.2 bitcast_dynamic-update-slice_fusion.6
  10.9 2.2 bitcast_dynamic-update-slice_fusion.6
  13.8 2.2 bitcast_dynamic-update-slice_fusion.6
  16.7 2.2 bitcast_dynamic-update-slice_fusion.6
  19.6 2.2 bitcast_dynamic-update-slice_fusion.6
  22.5 2.2 bitcast_dynamic-update-slice_fusion.6
  25.4 2.2 bitcast_dynamic-update-slice_fusion.6
  28.2 2.2 bitcast_dynamic-update-slice_fusion.6
  31.1 2.2 bitcast_dynamic-update-slice_fusion.6
  34.0 2.2 bitcast_dynamic-update-slice_fusion.6
  36.9 2.2 bitcast_dynamic-update-slice_fusion.6
  39.8 2.2 bitcast_dynamic-update-slice_fusion.6
  42.7 2.2 bitcast_dynamic-update-slice_fusion.6
  51.3 2.2 bitcast_dynamic-update-slice_fusion.6
  54.2 2.2 bitcast_dynamic-update-slice_fusion.6
  57.1 2.2 bitcast_dynamic-update-slice_fusion.6
  60.0 2.2 bitcast_dynamic-update-slice_fusion.6
  62.9 2.2 bitcast_dynamic-update-slice_fusion.6
  65.8 2.2 bitcast_dynamic-update-slice_fusion.6
  68.7 2.2 bitcast_dynamic-update-slice_fusion.6
  71.6 2.2 bitcast_dynamic-update-slice_fusion.6
  94.6 3.5 fusion.76
  100.2 8.6 %all-to-all-start = ((f32[32,1,64,128]{3,2,1,0:T(8,128)}), f32[32,1,64,128]{3,2,1,0:T(8,128)S(1)}, u32[]{:S(2)}, u32[]{:S(2)}) async-start(f32[32,1,64,128]{3,2,1,0:T(8,128)} %fusion.68), calls=%async_computation | async-start | bytes 2097152 | tf_op jit(solution)/shard_map/all_to_all | solution.py:235
  115.6 64.4 %all-reduce.3 = (f32[32]{0:T(128)S(1)}, f32[32]{0:T(128)S(1)}) all-reduce(f32[32]{0:T(128)S(1)} %bitcast_dynamic-update-slice_fusion.3, f32[32]{0:T(128)S(1)} %bitcast_dynamic-update-slice_fusion.2), channel_id=1, replica_groups=mesh['tomo'=8,'tilt'=32] {'tilt'}, use_global_device_ids=true, to_apply=%add | all-reduce | flops 64 | bytes 512
  183.8 20.8 %all_gather.10 = f32[1,32,6]{2,0,1:T(1,128)S(1)} all-gather(f32[1,1,6]{2,0,1:T(1,128)S(1)} %bitcast.220), channel_id=1, replica_groups=mesh['tomo'=8,'tilt'=32] {'tilt'}, dimensions={1}, use_global_device_ids=true | all-gather | bytes 792 | tf_op jit(solution)/shard_map/all_gather | solution.py:239
  204.7 3.5 sine_negate_fusion
  208.8 306.5 %while.17 = (s32[]{:T(128)}, f32[5,2048]{1,0:T(8,128)S(1)}, f32[8,4,6]{2,1,0:T(4,128)S(1)}, f32[8,4,2,3]{1,2,3,0:T(2,128)S(1)}, f32[8,4,6]{2,1,0:T(4,128)S(1)}, ...) while((s32[]{:T(128)}, f32[5,2048]{1,0:T(8,128)S(1)}, ...), condition=%wide.region_13.14_spmd.clone.clone, body=%wide.region_1.13_spmd.clone.clone.sunk | while | flops 845012160 | bytes 39035212 | solution.py:179
  210.4 15.4 %fusion.154 = (bf16[4,64,2048]{2,1,0:T(8,128)(2,1)S(1)}, bf16[4,64,2048]{2,1,0:T(8,128)(2,1)S(1)}, bf16[4,64,2048]{2,1,0:T(8,128)(2,1)S(1)}, bf16[4,64,2048]{2,1,0:T(8,128)(2,1)S(1)}) fusion(f32[64,2048]{1,0:T(8,128)S(1)} %get-tuple-element.519, f32[4,2048]{1,0:T(4,128)S(1)} %get-tuple-element.522, f32[64]{0:T(128)S(1)} %broadcast_multiply_fusion.7, ...), kind=kLoop, calls=%fused_computation.25.clone.1 | loop fusion | flops 5242880 | bytes 6357248 | tf_op jit(solution)/shard_map/convert.2
  228.6 16.9 %fusion.162 = (f32[4,2048]{1,0:T(4,128)S(1)}, f32[4,2048]{1,0:T(4,128)S(1)}, f32[4,2048]{1,0:T(4,128)S(1)}, f32[4,2048]{1,0:T(4,128)S(1)}) fusion(f32[4,128,2048]{2,1,0:T(8,128)S(1)} %fusion.158, f32[64,2048]{1,0:T(8,128)S(1)} %get-tuple-element.519, f32[4,2048]{1,0:T(4,128)S(1)} %get-tuple-element.522, f32[64]{0:T(128)S(1)} %broadcast_multiply_fusion.7, ...), kind=kLoop, calls=%fused_computation.17.clone.1 | loop fusion | flops 13598720 | bytes 10683136 | tf_op jit(solution)/shard_map/while/body/eval_jaxpr/vmap()/reduce_sum | solution.py:121
  248.7 15.4 %fusion.154 = (bf16[4,64,2048]{2,1,0:T(8,128)(2,1)S(1)}, bf16[4,64,2048]{2,1,0:T(8,128)(2,1)S(1)}, bf16[4,64,2048]{2,1,0:T(8,128)(2,1)S(1)}, bf16[4,64,2048]{2,1,0:T(8,128)(2,1)S(1)}) fusion(f32[64,2048]{1,0:T(8,128)S(1)} %get-tuple-element.519, f32[4,2048]{1,0:T(4,128)S(1)} %get-tuple-element.522, f32[64]{0:T(128)S(1)} %broadcast_multiply_fusion.7, ...), kind=kLoop, calls=%fused_computation.25.clone.1 | loop fusion | flops 5242880 | bytes 6357248 | tf_op jit(solution)/shard_map/convert.2
  266.9 16.9 %fusion.162 = (f32[4,2048]{1,0:T(4,128)S(1)}, f32[4,2048]{1,0:T(4,128)S(1)}, f32[4,2048]{1,0:T(4,128)S(1)}, f32[4,2048]{1,0:T(4,128)S(1)}) fusion(f32[4,128,2048]{2,1,0:T(8,128)S(1)} %fusion.158, f32[64,2048]{1,0:T(8,128)S(1)} %get-tuple-element.519, f32[4,2048]{1,0:T(4,128)S(1)} %get-tuple-element.522, f32[64]{0:T(128)S(1)} %broadcast_multiply_fusion.7, ...), kind=kLoop, calls=%fused_computation.17.clone.1 | loop fusion | flops 13598720 | bytes 10683136 | tf_op jit(solution)/shard_map/while/body/eval_jaxpr/vmap()/reduce_sum | solution.py:121
  287.0 15.4 %fusion.154 = (bf16[4,64,2048]{2,1,0:T(8,128)(2,1)S(1)}, bf16[4,64,2048]{2,1,0:T(8,128)(2,1)S(1)}, bf16[4,64,2048]{2,1,0:T(8,128)(2,1)S(1)}, bf16[4,64,2048]{2,1,0:T(8,128)(2,1)S(1)}) fusion(f32[64,2048]{1,0:T(8,128)S(1)} %get-tuple-element.519, f32[4,2048]{1,0:T(4,128)S(1)} %get-tuple-element.522, f32[64]{0:T(128)S(1)} %broadcast_multiply_fusion.7, ...), kind=kLoop, calls=%fused_computation.25.clone.1 | loop fusion | flops 5242880 | bytes 6357248 | tf_op jit(solution)/shard_map/convert.2
  305.2 16.9 %fusion.162 = (f32[4,2048]{1,0:T(4,128)S(1)}, f32[4,2048]{1,0:T(4,128)S(1)}, f32[4,2048]{1,0:T(4,128)S(1)}, f32[4,2048]{1,0:T(4,128)S(1)}) fusion(f32[4,128,2048]{2,1,0:T(8,128)S(1)} %fusion.158, f32[64,2048]{1,0:T(8,128)S(1)} %get-tuple-element.519, f32[4,2048]{1,0:T(4,128)S(1)} %get-tuple-element.522, f32[64]{0:T(128)S(1)} %broadcast_multiply_fusion.7, ...), kind=kLoop, calls=%fused_computation.17.clone.1 | loop fusion | flops 13598720 | bytes 10683136 | tf_op jit(solution)/shard_map/while/body/eval_jaxpr/vmap()/reduce_sum | solution.py:121
  325.3 15.4 %fusion.154 = (bf16[4,64,2048]{2,1,0:T(8,128)(2,1)S(1)}, bf16[4,64,2048]{2,1,0:T(8,128)(2,1)S(1)}, bf16[4,64,2048]{2,1,0:T(8,128)(2,1)S(1)}, bf16[4,64,2048]{2,1,0:T(8,128)(2,1)S(1)}) fusion(f32[64,2048]{1,0:T(8,128)S(1)} %get-tuple-element.519, f32[4,2048]{1,0:T(4,128)S(1)} %get-tuple-element.522, f32[64]{0:T(128)S(1)} %broadcast_multiply_fusion.7, ...), kind=kLoop, calls=%fused_computation.25.clone.1 | loop fusion | flops 5242880 | bytes 6357248 | tf_op jit(solution)/shard_map/convert.2
  343.5 16.9 %fusion.162 = (f32[4,2048]{1,0:T(4,128)S(1)}, f32[4,2048]{1,0:T(4,128)S(1)}, f32[4,2048]{1,0:T(4,128)S(1)}, f32[4,2048]{1,0:T(4,128)S(1)}) fusion(f32[4,128,2048]{2,1,0:T(8,128)S(1)} %fusion.158, f32[64,2048]{1,0:T(8,128)S(1)} %get-tuple-element.519, f32[4,2048]{1,0:T(4,128)S(1)} %get-tuple-element.522, f32[64]{0:T(128)S(1)} %broadcast_multiply_fusion.7, ...), kind=kLoop, calls=%fused_computation.17.clone.1 | loop fusion | flops 13598720 | bytes 10683136 | tf_op jit(solution)/shard_map/while/body/eval_jaxpr/vmap()/reduce_sum | solution.py:121
  363.6 15.4 %fusion.154 = (bf16[4,64,2048]{2,1,0:T(8,128)(2,1)S(1)}, bf16[4,64,2048]{2,1,0:T(8,128)(2,1)S(1)}, bf16[4,64,2048]{2,1,0:T(8,128)(2,1)S(1)}, bf16[4,64,2048]{2,1,0:T(8,128)(2,1)S(1)}) fusion(f32[64,2048]{1,0:T(8,128)S(1)} %get-tuple-element.519, f32[4,2048]{1,0:T(4,128)S(1)} %get-tuple-element.522, f32[64]{0:T(128)S(1)} %broadcast_multiply_fusion.7, ...), kind=kLoop, calls=%fused_computation.25.clone.1 | loop fusion | flops 5242880 | bytes 6357248 | tf_op jit(solution)/shard_map/convert.2
  381.8 16.9 %fusion.162 = (f32[4,2048]{1,0:T(4,128)S(1)}, f32[4,2048]{1,0:T(4,128)S(1)}, f32[4,2048]{1,0:T(4,128)S(1)}, f32[4,2048]{1,0:T(4,128)S(1)}) fusion(f32[4,128,2048]{2,1,0:T(8,128)S(1)} %fusion.158, f32[64,2048]{1,0:T(8,128)S(1)} %get-tuple-element.519, f32[4,2048]{1,0:T(4,128)S(1)} %get-tuple-element.522, f32[64]{0:T(128)S(1)} %broadcast_multiply_fusion.7, ...), kind=kLoop, calls=%fused_computation.17.clone.1 | loop fusion | flops 13598720 | bytes 10683136 | tf_op jit(solution)/shard_map/while/body/eval_jaxpr/vmap()/reduce_sum | solution.py:121
  401.9 15.4 %fusion.154 = (bf16[4,64,2048]{2,1,0:T(8,128)(2,1)S(1)}, bf16[4,64,2048]{2,1,0:T(8,128)(2,1)S(1)}, bf16[4,64,2048]{2,1,0:T(8,128)(2,1)S(1)}, bf16[4,64,2048]{2,1,0:T(8,128)(2,1)S(1)}) fusion(f32[64,2048]{1,0:T(8,128)S(1)} %get-tuple-element.519, f32[4,2048]{1,0:T(4,128)S(1)} %get-tuple-element.522, f32[64]{0:T(128)S(1)} %broadcast_multiply_fusion.7, ...), kind=kLoop, calls=%fused_computation.25.clone.1 | loop fusion | flops 5242880 | bytes 6357248 | tf_op jit(solution)/shard_map/convert.2
  420.1 16.9 %fusion.162 = (f32[4,2048]{1,0:T(4,128)S(1)}, f32[4,2048]{1,0:T(4,128)S(1)}, f32[4,2048]{1,0:T(4,128)S(1)}, f32[4,2048]{1,0:T(4,128)S(1)}) fusion(f32[4,128,2048]{2,1,0:T(8,128)S(1)} %fusion.158, f32[64,2048]{1,0:T(8,128)S(1)} %get-tuple-element.519, f32[4,2048]{1,0:T(4,128)S(1)} %get-tuple-element.522, f32[64]{0:T(128)S(1)} %broadcast_multiply_fusion.7, ...), kind=kLoop, calls=%fused_computation.17.clone.1 | loop fusion | flops 13598720 | bytes 10683136 | tf_op jit(solution)/shard_map/while/body/eval_jaxpr/vmap()/reduce_sum | solution.py:121
  440.2 15.4 %fusion.154 = (bf16[4,64,2048]{2,1,0:T(8,128)(2,1)S(1)}, bf16[4,64,2048]{2,1,0:T(8,128)(2,1)S(1)}, bf16[4,64,2048]{2,1,0:T(8,128)(2,1)S(1)}, bf16[4,64,2048]{2,1,0:T(8,128)(2,1)S(1)}) fusion(f32[64,2048]{1,0:T(8,128)S(1)} %get-tuple-element.519, f32[4,2048]{1,0:T(4,128)S(1)} %get-tuple-element.522, f32[64]{0:T(128)S(1)} %broadcast_multiply_fusion.7, ...), kind=kLoop, calls=%fused_computation.25.clone.1 | loop fusion | flops 5242880 | bytes 6357248 | tf_op jit(solution)/shard_map/convert.2
  458.4 16.9 %fusion.162 = (f32[4,2048]{1,0:T(4,128)S(1)}, f32[4,2048]{1,0:T(4,128)S(1)}, f32[4,2048]{1,0:T(4,128)S(1)}, f32[4,2048]{1,0:T(4,128)S(1)}) fusion(f32[4,128,2048]{2,1,0:T(8,128)S(1)} %fusion.158, f32[64,2048]{1,0:T(8,128)S(1)} %get-tuple-element.519, f32[4,2048]{1,0:T(4,128)S(1)} %get-tuple-element.522, f32[64]{0:T(128)S(1)} %broadcast_multiply_fusion.7, ...), kind=kLoop, calls=%fused_computation.17.clone.1 | loop fusion | flops 13598720 | bytes 10683136 | tf_op jit(solution)/shard_map/while/body/eval_jaxpr/vmap()/reduce_sum | solution.py:121
  478.5 15.4 %fusion.154 = (bf16[4,64,2048]{2,1,0:T(8,128)(2,1)S(1)}, bf16[4,64,2048]{2,1,0:T(8,128)(2,1)S(1)}, bf16[4,64,2048]{2,1,0:T(8,128)(2,1)S(1)}, bf16[4,64,2048]{2,1,0:T(8,128)(2,1)S(1)}) fusion(f32[64,2048]{1,0:T(8,128)S(1)} %get-tuple-element.519, f32[4,2048]{1,0:T(4,128)S(1)} %get-tuple-element.522, f32[64]{0:T(128)S(1)} %broadcast_multiply_fusion.7, ...), kind=kLoop, calls=%fused_computation.25.clone.1 | loop fusion | flops 5242880 | bytes 6357248 | tf_op jit(solution)/shard_map/convert.2
  496.7 16.9 %fusion.162 = (f32[4,2048]{1,0:T(4,128)S(1)}, f32[4,2048]{1,0:T(4,128)S(1)}, f32[4,2048]{1,0:T(4,128)S(1)}, f32[4,2048]{1,0:T(4,128)S(1)}) fusion(f32[4,128,2048]{2,1,0:T(8,128)S(1)} %fusion.158, f32[64,2048]{1,0:T(8,128)S(1)} %get-tuple-element.519, f32[4,2048]{1,0:T(4,128)S(1)} %get-tuple-element.522, f32[64]{0:T(128)S(1)} %broadcast_multiply_fusion.7, ...), kind=kLoop, calls=%fused_computation.17.clone.1 | loop fusion | flops 13598720 | bytes 10683136 | tf_op jit(solution)/shard_map/while/body/eval_jaxpr/vmap()/reduce_sum | solution.py:121
  515.2 79.2 %psum.7 = f32[5,2048]{1,0:T(8,128)} all-reduce(f32[5,2048]{1,0:T(8,128)S(1)} %get-tuple-element.138), channel_id=1, replica_groups=mesh['tomo'=8,'tilt'=32] {'tomo','tilt'}, use_global_device_ids=true, to_apply=%region_14.15 | all-reduce | flops 10240 | bytes 81920 | tf_op jit(solution)/shard_map/psum | solution.py:255
  594.5 121.1 %all-reduce.2 = f32[32,6]{1,0:T(8,128)S(1)} all-reduce(f32[32,6]{1,0:T(8,128)S(1)} %bitcast.217), channel_id=2, replica_groups=mesh['tomo'=8,'tilt'=32] {'tilt'}, use_global_device_ids=true, to_apply=%region_15.16.clone | all-reduce | flops 192 | bytes 1536
  (442 shorter events, 97.5 us)
Async XLA Ops:
  98.8 10.0 %copy-start.5 = (f32[1,3,32]{2,0,1:T(1,128)S(1)}, f32[1,3,32]{2,0,1:T(1,128)}, u32[]{:S(2)}) copy-start(f32[1,3,32]{2,0,1:T(1,128)} %param.13) | copy-start | bytes 1156
  98.8 14.9 %copy-start.6 = (u32[256]{0:T(256)S(1)}, u32[256]{0:T(256)}, u32[]{:S(2)}) copy-start(u32[256]{0:T(256)} %constant.123) | copy-start | bytes 3076
  98.8 83.1 %copy-start.3 = (f32[32,1,3]{0,2,1:T(4,128)S(1)}, f32[32,1,3]{0,2,1:T(4,128)}, u32[]{:S(2)}) copy-start(f32[32,1,3]{0,2,1:T(4,128)} %constant.97.clone.1) | copy-start | bytes 1156
  98.8 83.1 %copy-start.4 = (f32[32,1,3]{0,2,1:T(4,128)S(1)}, f32[32,1,3]{0,2,1:T(4,128)}, u32[]{:S(2)}) copy-start(f32[32,1,3]{0,2,1:T(4,128)} %constant.98.clone.1) | copy-start | bytes 1156
  100.2 83.6 %copy-start.2 = (f32[2048]{0:T(1024)S(1)}, f32[2048]{0:T(1024)}, u32[]{:S(2)}) copy-start(f32[2048]{0:T(1024)} %param.19) | copy-start | bytes 24580
  100.2 83.6 %copy-start = (f32[2048]{0:T(1024)S(1)}, f32[2048]{0:T(1024)}, u32[]{:S(2)}) copy-start(f32[2048]{0:T(1024)} %param.18) | copy-start | bytes 24580
  100.2 83.6 %copy-start.7 = (f32[1,1,6]{2,1,0:T(1,128)S(1)}, f32[1,1,6]{2,1,0:T(1,128)}, u32[]{:S(2)}) copy-start(f32[1,1,6]{2,1,0:T(1,128)} %param.16) | copy-start | bytes 76
  100.2 108.1 %all-to-all-start = ((f32[32,1,64,128]{3,2,1,0:T(8,128)}), f32[32,1,64,128]{3,2,1,0:T(8,128)S(1)}, u32[]{:S(2)}, u32[]{:S(2)}) async-start(f32[32,1,64,128]{3,2,1,0:T(8,128)} %fusion.68), calls=%async_computation | async-start | bytes 2097152 | tf_op jit(solution)/shard_map/all_to_all | solution.py:235
  204.7 4.0 copy-start.1
where the time goes:
time: 723 us; the launch traced here: 717 us
  blocking collectives  286 us (40%)
  other arithmetic  275 us (38%)
  local copies, waits for them, and re-layouts  101 us (14%)
  matrix products  37.6 us (5%)
  starting transfers between devices  8.63 us (1%)
    unnamed x2, blocking collectives  185 us
    reduce_sum x8, other arithmetic, slice_terms(): jnp.sum(freq_col * (slice_xi * back_xr - slice_xr * back_xi), 0)  135 us
    another operation x8, other arithmetic  123 us
    gather x96, local copies, waits for them, and re-layouts  91.9 us
    psum x1, blocking collectives, on_device(): template = lax.psum(template, ('tomo', 'tilt'))  79.2 us
    all_gather x1, blocking collectives, on_device(): lax.all_gather(warp, 'tilt', axis=1, tiled=True)  20.8 us
  transfers between devices with their start and end apart: 1, of which 0 were waited for; matrix products, arithmetic and copies ran while one was open for 1% of the time, Pallas kernels for 0%

commit v1 on v0

v1 whole, which is shorter than its diff:
```python
import math

import jax
import jax.numpy as jnp
import numpy as np
from jax import lax
from jax.experimental import pallas as pl
from jax.experimental.pallas import tpu as pltpu
from jax.sharding import PartitionSpec as P

G = 2048
BOX = 64
IMG = 1024
NT = 32
NP = 32
CH = 256
NCH = G // CH
HALF = 40
ROWS = 2 * HALF
F32 = jnp.float32
BF16 = jnp.bfloat16


def _fit(fn, degree):
    n = 64
    nodes = 0.125 * (1 + np.cos(np.pi * (np.arange(n) + 0.5) / n))
    return [float(c) for c in np.polynomial.polynomial.polyfit(nodes, fn(np.sqrt(nodes)), degree)]


SIN_POLY = _fit(lambda u: np.sin(np.pi * u) / u, 5)
COS_POLY = _fit(lambda u: np.cos(np.pi * u), 5)


def _horner(w, coefs):
    acc = jnp.full_like(w, coefs[-1])
    for c in coefs[-2::-1]:
        acc = acc * w + c
    return acc


def cos_sin_turns(turns):
    u = turns - jnp.round(turns)
    w = u * u
    s = u * _horner(w, SIN_POLY)
    c = _horner(w, COS_POLY)
    return 1.0 - 2.0 * (s * s), 2.0 * (s * c)


def split(x):
    hi = x.astype(BF16)
    return hi, (x - hi.astype(F32)).astype(BF16)


def np_split(x):
    hi = x.astype(jnp.bfloat16)
    lo = (x - hi.astype(np.float64)).astype(jnp.bfloat16)
    return hi, lo


def tables():
    pos = np.arange(BOX)
    freq = np.arange(33)
    ang = 2 * np.pi * ((pos[:, None] * freq[None, :]) % BOX) / BOX
    lanes = np.zeros((BOX, 128))
    lanes[:, :33] = np.cos(ang)
    lanes[:, 64:97] = np.sin(ang)
    right = np.zeros((128, 256))
    right[:64, :128] = lanes
    right[64:, 128:] = lanes
    right_hi, right_lo = np_split(right)
    rows = np.zeros((ROWS, BOX))
    rows[:33] = np.cos(ang).T / BOX
    rows[HALF : HALF + 33] = np.sin(ang).T / BOX
    left_hi, left_lo = np_split(rows)
    left = np.concatenate([left_hi, left_hi, left_lo], 1)
    phi = np.ones(33)
    phi[0] = phi[32] = 0.5
    both = -4.0 / (NT * NP) * phi[:, None] * phi[None, :]
    plus, minus = both.copy(), both.copy()
    plus[32, 32] *= 2.0
    minus[32, 32] = 0.0
    aux = np.zeros((3, HALF, 128), np.float32)
    for base in (0, 64):
        aux[0, :33, base : base + 33] = freq[:, None] ** 2 + freq[None, :] ** 2
        aux[1, :33, base : base + 33] = plus
        aux[2, :33, base : base + 33] = minus
    return right_hi, right_lo, left, aux


def cut_kernel(anchor, angle, focus, warp, image, out):
    lane = lax.broadcasted_iota(jnp.int32, (8, 128), 1)
    sub = lax.broadcasted_iota(jnp.int32, (8, 128), 0)
    values = [angle[0, 0], focus[0, 0]] + [warp[0, 0, i] for i in range(6)]
    row = jnp.zeros((8, 128), F32)
    for i, v in enumerate(values):
        row = jnp.where(lane == i, v, row)
    hi = row.astype(BF16).astype(F32)
    mid = (row - hi).astype(BF16).astype(F32)
    low = row - hi - mid
    parts = jnp.where(sub == 0, hi, jnp.where(sub == 1, mid, jnp.where(sub == 2, low, 0.0)))
    parts = parts.astype(BF16)
    col_at = lax.broadcasted_iota(jnp.int32, (256, 128), 0)
    col_of = lax.broadcasted_iota(jnp.int32, (256, 128), 1) % BOX
    row_at = lax.broadcasted_iota(jnp.int32, (BOX, 80), 1)
    row_of = lax.broadcasted_iota(jnp.int32, (BOX, 80), 0)
    left_half = lax.broadcasted_iota(jnp.int32, (32, 128), 1) < BOX

    def one(p, carry):
        r, c = anchor[0, 0, p, 0], anchor[0, 0, p, 1]
        r0 = pl.multiple_of(jnp.minimum((r // 16) * 16, IMG - 80), 16)
        c0 = pl.multiple_of(jnp.minimum((c // 128) * 128, IMG - 256), 128)
        window = image[0, 0, pl.ds(r0, 80), pl.ds(c0, 256)]
        pick_col = jnp.where(col_at == col_of + (c - c0), 1.0, 0.0).astype(BF16)
        pick_row = jnp.where(row_at == row_of + (r - r0), 1.0, 0.0).astype(BF16)
        strip = jnp.dot(window, pick_col, preferred_element_type=F32).astype(BF16)
        patch = jnp.dot(pick_row, strip, preferred_element_type=F32)
        packed = jnp.where(left_half, patch[:32], patch[32:]).astype(BF16)
        out[p] = jnp.concatenate([packed, parts], 0)
        return carry

    lax.fori_loop(0, NP, one, 0, unroll=4)


def cut(images, anchors, angle, focus, warp):
    smem = pl.BlockSpec(memory_space=pltpu.SMEM)
    vmem = pl.BlockSpec(memory_space=pltpu.VMEM)
    return pl.pallas_call(
        cut_kernel,
        out_shape=jax.ShapeDtypeStruct((NP, 40, 128), BF16),
        in_specs=[smem, smem, smem, smem, vmem],
        out_specs=vmem,
        compiler_params=pltpu.CompilerParams(vmem_limit_bytes=16 << 20),
    )(anchors, angle, focus, warp, images)


def work_kernel(
    slot,
    euler,
    received,
    centers,
    amplitudes,
    widths,
    right_hi,
    right_lo,
    left,
    aux,
    out,
    xs,
    base,
    step,
    nyq,
    nyqk,
    env,
    acc,
    model,
    spectra,
    mats,
    zsc,
):
    prm = jnp.sum(received[:, 32:40, :].astype(F32), axis=1)
    ct, st = cos_sin_turns(prm * (0.5 / math.pi))
    ct, st = ct[:, 0:1], st[:, 0:1]
    a00, a01 = 1.0 + prm[:, 2:3], prm[:, 3:4]
    a10, a11 = prm[:, 4:5], 1.0 + prm[:, 5:6]
    sh_x, sh_y = 20.0 * prm[:, 6:7], 20.0 * prm[:, 7:8]
    mine = slot[0]
    turn = []
    for i in range(3):
        angle = jnp.full((8, 128), euler[0, i, mine], F32)
        c, s = cos_sin_turns(angle * (0.5 / math.pi))
        turn.append((c[0:1, 0:1], s[0:1, 0:1]))
    (ca, sa), (cb, sb), (cc, sc) = turn

    def rotated(sl):
        x, y, z = centers[0:1, sl], centers[1:2, sl], centers[2:3, sl]
        x, y = cc * x - sc * y, sc * x + cc * y
        x, z = cb * x + sb * z, cb * z - sb * x
        x, y = ca * x - sa * y, sa * x + ca * y
        return x, y, z

    blur = 2.0 * math.pi**2 / BOX**2
    freq8 = lax.broadcasted_iota(jnp.int32, (8, CH), 0).astype(F32)
    freq32 = lax.broadcasted_iota(jnp.int32, (32, CH), 0).astype(F32)
    first = lax.broadcasted_iota(jnp.int32, (8, CH), 0) == 0

    def prepare(c, carry):
        sl = pl.ds(pl.multiple_of(c * CH, CH), CH)
        r0, r1, r2 = rotated(sl)
        px = ct * r0 + st * r2
        ux = (a00 * px + a01 * r1 + sh_x) * (1.0 / BOX) + 0.5
        uy = (a10 * px + a11 * r1 + sh_y) * (1.0 / BOX) + 0.5
        wide = -blur * widths[0:1, sl] * widths[0:1, sl]
        damp = jnp.exp(wide * (freq32 * freq32))
        env[0, :, sl] = damp
        env[1, :, sl] = amplitudes[0:1, sl] * damp
        damp32 = jnp.exp(wide * 1024.0)
        for axis, u in ((0, ux), (1, uy)):
            u = u - jnp.round(u)
            c1, s1 = cos_sin_turns(u)
            c8, s8 = cos_sin_turns(8.0 * u)
            cn, sn = cos_sin_turns(32.0 * u)
            d32 = damp32 if axis == 0 else amplitudes[0:1, sl] * damp32
            nyq[2 * axis, :, sl] = cn * d32
            nyq[2 * axis + 1, :, sl] = sn * d32
            step[2 * axis, :, sl] = c8
            step[2 * axis + 1, :, sl] = s8

            def times(p, q):
                return p[0] * q[0] - p[1] * q[1], p[0] * q[1] + p[1] * q[0]

            e1 = (c1, s1)
            e2 = times(e1, e1)
            e3 = times(e2, e1)
            e4 = times(e2, e2)
            e5 = times(e4, e1)
            e6 = times(e3, e3)
            e7 = times(e4, e3)
            e0 = (jnp.ones_like(c1), jnp.zeros_like(c1))
            for j, e in enumerate((e0, e1, e2, e3, e4, e5, e6, e7)):
                for i in range(CH // 128):
                    tile = c * (CH // 128) + i
                    lanes = slice(i * 128, i * 128 + 128)
                    base[2 * axis, tile, pl.ds(j, NT, stride=8), :] = e[0][:, lanes]
                    base[2 * axis + 1, tile, pl.ds(j, NT, stride=8), :] = e[1][:, lanes]
        return carry

    lax.fori_loop(0, NCH, prepare, 0)

    def stacked(groups_c, groups_s, k, axis, sl):
        cn = jnp.where(first, nyq[2 * axis, pl.ds(k, 1), sl], 0.0)
        sn = jnp.where(first, nyq[2 * axis + 1, pl.ds(k, 1), sl], 0.0)
        return jnp.concatenate(groups_c + [cn] + groups_s + [sn], 0).astype(BF16)

    def forward(k, carry):
        k8 = pl.multiple_of(k * 8, 8)
        total = jnp.zeros((ROWS, ROWS), F32)
        for c in range(NCH):
            sl = slice(c * CH, (c + 1) * CH)
            sides = []
            for axis in (0, 1):
                tiles = range(c * (CH // 128), (c + 1) * (CH // 128))
                gc = jnp.concatenate([base[2 * axis, t, pl.ds(k8, 8), :] for t in tiles], 1)
                gs = jnp.concatenate([base[2 * axis + 1, t, pl.ds(k8, 8), :] for t in tiles], 1)
                rc = step[2 * axis, pl.ds(k, 1), sl]
                rs = step[2 * axis + 1, pl.ds(k, 1), sl]
                cs, ss = [], []
                for m in range(4):
                    damp = env[axis, 8 * m : 8 * m + 8, sl]
                    cm, sm = damp * gc, damp * gs
                    xs[k, axis * 64 + 8 * m : axis * 64 + 8 * m + 8, sl] = cm
                    xs[k, axis * 64 + 32 + 8 * m : axis * 64 + 40 + 8 * m, sl] = sm
                    cs.append(cm)
                    ss.append(sm)
                    if m < 3:
                        gc, gs = gc * rc - gs * rs, gc * rs + gs * rc
                sides.append(stacked(cs, ss, k, axis, sl))
            total = total + lax.dot_general(
                sides[0], sides[1], (((1,), (1,)), ((), ())), preferred_element_type=F32
            )
        model[k, :, 0:ROWS] = total
        return carry

    lax.fori_loop(0, NT, forward, 0)

    for b in range(4):
        rows = received[8 * b : 8 * b + 8, 0:32, :].reshape(256, 128)
        zsc[256 * b : 256 * b + 256, :] = jnp.dot(
            rows, right_hi[...], preferred_element_type=F32
        ) + jnp.dot(rows, right_lo[...], preferred_element_type=F32)

    lane = lax.broadcasted_iota(jnp.int32, (HALF, 128), 1)
    sign = jnp.where(lane < 64, 1.0, -1.0)

    def swap(x):
        return pltpu.roll(x, 64, 1)

    def spectrum(k, sums):
        z = zsc[pl.ds(pl.multiple_of(k * 32, 32), 32), :]
        z = jnp.concatenate([z[:, :128], z[:, 128:]], 0)
        z_hi, z_lo = split(z)
        p = jnp.dot(left[...], jnp.concatenate([z_hi, z_lo, z_hi], 0), preferred_element_type=F32)
        pc, ps = p[:HALF], swap(p[HALF:])
        spectra[k, :HALF] = pc
        spectra[k, HALF:] = ps
        plus, minus = sign * pc - ps, pc + sign * ps
        return sums[0] + plus * plus, sums[1] + minus * minus

    nought = jnp.zeros((HALF, 128), F32)
    plus, minus = lax.fori_loop(0, NT, spectrum, (nought, nought), unroll=2)
    f_plus = aux[1] / (0.25 + (plus + swap(plus)) * (1.0 / NT))
    f_minus = aux[2] / (0.25 + (minus + swap(minus)) * (1.0 / NT))
    radius = aux[0]

    def spread(x):
        return jnp.where(lane < HALF, x, pltpu.roll(x, 24, 1))

    def gather(x):
        return jnp.where(lane < HALF, x, pltpu.roll(x, 104, 1))

    lane_r = lax.broadcasted_iota(jnp.int32, (ROWS, 128), 1)

    def joined(first_part, second_part):
        moved = pltpu.roll(second_part, ROWS, 1)
        return jnp.where(lane_r < ROWS, first_part, moved), jnp.where(lane_r < 32, moved, 0.0)

    def flipped(x):
        square = jnp.concatenate([x, jnp.zeros((128 - ROWS, 128), F32)], 0)
        return jnp.transpose(square)[:ROWS]

    model[:, :, ROWS:128] = jnp.zeros((NT, ROWS, 128 - ROWS), F32)

    def residual(k, carry):
        focus = jnp.sum(received[k, 32:40, 0:128].astype(F32), axis=0, keepdims=True)[:, 1:2]
        x = focus * radius * (1.0 / BOX) + 0.1
        n = jnp.round(x * (0.5 / math.pi))
        r = (x - n * 6.28125) - n * (2.0 * math.pi - 6.28125)
        ctf = -cos_sin_turns(r * (0.5 / math.pi))[1]
        tc = spread(model[k, :HALF])
        ts = swap(spread(model[k, HALF:]))
        dc = spectra[k, :HALF] - ctf * tc
        ds = spectra[k, HALF:] - ctf * ts
        hp = (f_plus * ctf) * (sign * dc - ds)
        hm = (f_minus * ctf) * (dc + sign * ds)
        m1 = jnp.concatenate([gather(hm), gather(swap(sign * hm))], 0)
        m2 = jnp.concatenate([gather(sign * hp), gather(-swap(hp))], 0)
        for i, (u, v) in enumerate(((m1, m2), (flipped(m1), flipped(m2)))):
            lo, hi = joined(u, v)
            mats[k, i, :, 0:128] = lo.astype(BF16)
            mats[k, i, :, 128:256] = hi.astype(BF16)
        return carry

    lax.fori_loop(0, NT, residual, 0)

    acc[...] = jnp.zeros_like(acc)
    w1 = [freq8 + float(8 * m) for m in range(4)]
    w2 = [w * w for w in w1]

    def backward(k, carry):
        k8 = pl.multiple_of(k * 8, 8)
        for c in range(NCH):
            sl = slice(c * CH, (c + 1) * CH)
            sides, parts = [], []
            for axis in (0, 1):
                cs = [xs[k, axis * 64 + 8 * m : axis * 64 + 8 * m + 8, sl] for m in range(4)]
                ss = [xs[k, axis * 64 + 32 + 8 * m : axis * 64 + 40 + 8 * m, sl] for m in range(4)]
                parts.append((cs, ss))
                sides.append(stacked(cs, ss, k, axis, sl))
            width_sum = acc[0, :, sl]
            for axis in (0, 1):
                other = sides[1 - axis]
                back = jnp.dot(
                    mats[k, axis, :, 0 : 2 * ROWS],
                    jnp.concatenate([other, other], 0),
                    preferred_element_type=F32,
                )
                cs, ss = parts[axis]
                move, value = None, None
                for m in range(4):
                    kc = back[8 * m : 8 * m + 8]
                    ks = back[HALF + 8 * m : HALF + 8 * m + 8]
                    re = cs[m] * kc + ss[m] * ks
                    im = cs[m] * ks - ss[m] * kc
                    width_sum = width_sum + w2[m] * re
                    move = w1[m] * im if move is None else move + w1[m] * im
                    value = re if value is None else value + re
                if axis == 1:
                    acc[1, :, sl] = acc[1, :, sl] + value
                for i in range(CH // 128):
                    base[axis, c * (CH // 128) + i, pl.ds(k8, 8), :] = move[:, i * 128 : i * 128 + 128]
                nyqk[2 * axis, pl.ds(k, 1), sl] = back[32:33]
                nyqk[2 * axis + 1, pl.ds(k, 1), sl] = back[HALF + 32 : HALF + 33]
            acc[0, :, sl] = width_sum
        return carry

    lax.fori_loop(0, NT, backward, 0)

    terms = [jnp.zeros((NT, 128), F32) for _ in range(6)]
    unit = 2.0 * math.pi / BOX
    for c in range(G // 128):
        sl = slice(c * 128, (c + 1) * 128)
        moves, ends = [], []
        for axis in (0, 1):
            move = base[axis, c, pl.ds(0, NT, stride=8), :]
            for j in range(1, 8):
                move = move + base[axis, c, pl.ds(j, NT, stride=8), :]
            nc, ns = nyq[2 * axis, :, sl], nyq[2 * axis + 1, :, sl]
            kc, ks = nyqk[2 * axis, :, sl], nyqk[2 * axis + 1, :, sl]
            moves.append(unit * (move + 32.0 * (nc * ks - ns * kc)))
            ends.append(jnp.sum(nc * kc + ns * ks, axis=0, keepdims=True))
        mx, my = moves
        r0, r1, r2 = rotated(sl)
        px = ct * r0 + st * r2
        for i, t in enumerate((mx * px, mx * r1, my * px, my * r1, mx, my)):
            terms[i] = terms[i] + t
        vx = a00 * mx + a10 * my
        vy = a01 * mx + a11 * my
        x = jnp.sum(ct * vx, axis=0, keepdims=True)
        z = jnp.sum(st * vx, axis=0, keepdims=True)
        y = jnp.sum(vy, axis=0, keepdims=True)
        x, y = ca * x + sa * y, ca * y - sa * x
        x, z = cb * x - sb * z, sb * x + cb * z
        x, y = cc * x + sc * y, cc * y - sc * x
        curve = jnp.sum(acc[0, :, sl], axis=0, keepdims=True) + 1024.0 * (ends[0] + ends[1])
        value = jnp.sum(acc[1, :, sl], axis=0, keepdims=True) + ends[1]
        out[2 * c, 0:1, :] = x
        out[2 * c, 1:2, :] = y
        out[2 * c, 2:3, :] = z
        out[2 * c + 1, 0:1, :] = value / amplitudes[0:1, sl]
        out[2 * c + 1, 1:2, :] = (-2.0 * blur) * widths[0:1, sl] * curve
        out[2 * c + 1, 2:3, :] = jnp.zeros((1, 128), F32)
    lane_w = lax.broadcasted_iota(jnp.int32, (NT, 128), 1)
    warp_rows = jnp.zeros((NT, 128), F32)
    for i in range(6):
        total = jnp.sum(terms[i], axis=1, keepdims=True) * (20.0 if i > 3 else 1.0)
        warp_rows = jnp.where(lane_w == i, total, warp_rows)
    for k in range(NT):
        out[k, 3:4, :] = warp_rows[k : k + 1]


def work(slot, euler, received, centers, amplitudes, widths):
    smem = pl.BlockSpec(memory_space=pltpu.SMEM)
    vmem = pl.BlockSpec(memory_space=pltpu.VMEM)
    right_hi, right_lo, left, aux = tables()
    return pl.pallas_call(
        work_kernel,
        out_shape=jax.ShapeDtypeStruct((NT, 4, 128), F32),
        in_specs=[smem, smem] + [vmem] * 8,
        out_specs=vmem,
        scratch_shapes=[
            pltpu.VMEM((NT, 128, G), F32),
            pltpu.VMEM((4, G // 128, NT * 8, 128), F32),
            pltpu.VMEM((4, NT, G), F32),
            pltpu.VMEM((4, NT, G), F32),
            pltpu.VMEM((4, NT, G), F32),
            pltpu.VMEM((2, 32, G), F32),
            pltpu.VMEM((2, 8, G), F32),
            pltpu.VMEM((NT, ROWS, 128), F32),
            pltpu.VMEM((NT, ROWS, 128), F32),
            pltpu.VMEM((NT, 2, ROWS, 256), BF16),
            pltpu.VMEM((1024, 256), F32),
        ],
        compiler_params=pltpu.CompilerParams(vmem_limit_bytes=60 << 20),
    )(
        slot,
        euler,
        received,
        centers,
        amplitudes.reshape(1, G),
        widths.reshape(1, G),
        jnp.asarray(right_hi),
        jnp.asarray(right_lo),
        jnp.asarray(left),
        jnp.asarray(aux),
    )


def on_device(tilt_images, anchors, euler, tilt_angle, defocus, warp, centers, amplitudes, widths):
    payload = cut(tilt_images, anchors, tilt_angle, defocus, warp)
    received = lax.all_to_all(payload, "tilt", split_axis=0, concat_axis=0, tiled=True)
    slot = lax.axis_index("tilt").astype(jnp.int32).reshape(1)
    partial = work(slot, euler, received, centers, amplitudes, widths)
    shares = lax.all_to_all(partial, "tilt", split_axis=0, concat_axis=0, tiled=True)
    own = jnp.sum(shares, 0)
    warp_local = own[3, :6]
    tomos = lax.all_to_all(
        jnp.broadcast_to(own[None], (8, 4, 128)), "tomo", split_axis=0, concat_axis=0, tiled=True
    )
    chunk = jnp.sum(tomos, 0)
    whole = lax.all_to_all(
        jnp.broadcast_to(chunk[None], (NT, 4, 128)), "tilt", split_axis=0, concat_axis=0, tiled=True
    )
    whole = whole.reshape(16, 2, 4, 128)
    rows = jnp.concatenate([whole[:, 0, 0:3], whole[:, 1, 0:2]], 1)
    template = jnp.transpose(rows, (1, 0, 2)).reshape(5, G)
    return (template, warp_local.reshape(1, 1, 6))


def solution(mesh):
    placed = (
        P("tomo", "tilt", None, None),
        P("tomo", "tilt", None, None),
        P("tomo", None, None),
        P("tomo", "tilt"),
        P("tomo", "tilt"),
        P("tomo", "tilt", None),
        P(),
        P(),
        P(),
    )
    return jax.shard_map(
        on_device,
        mesh=mesh,
        in_specs=placed,
        out_specs=(P(), P("tomo", "tilt", None)),
        check_vma=False,
    )
```

time: 723 us -> 120 us (0.17)
  other arithmetic: 275 us -> 0.07 us
  blocking collectives: 286 us -> 25.8 us
  local copies, waits for them, and re-layouts: 101 us -> 6.16 us
  Pallas kernels: 0 us -> 55.6 us
  matrix products: 37.6 us -> 0 us
  waiting for transfers between devices: 0.01 us -> 15.9 us
    unnamed x2 -> x0, blocking collectives: 185 us -> none
    reduce_sum x25 -> x2, other arithmetic: 138 us -> 0.06 us  [the longest x1 0.04 us: on_device(): own = jnp.sum(shares, 0)]
    another operation x19 -> x0, other arithmetic: 123 us -> none
    gather x96 -> x0, local copies, waits for them, and re-layouts: 91.9 us -> none
    psum x1 -> x0, blocking collectives: 79.2 us -> none  [on_device(): template = lax.psum(template, ('tomo', 'tilt'))]
    pallas_call x0 -> x2, Pallas kernels: none -> 55.6 us  [the longest x1 49.2 us: work(): pl.pallas_call(work_kernel, out_shape=jax.ShapeDtypeStruct((NT, 4, 128),...]
    dot_general x61 -> x0, matrix products: 37.6 us -> none  [the longest x8 7.28 us: slice_terms(): blocks = jnp.dot(stack_x, stack_y.T, preferred_element_type=jnp.float32)]
    all_to_all x0 -> x2, blocking collectives: none -> 25.8 us  [the longest x1 14.6 us: on_device(): lax.all_to_all(jnp.broadcast_to(own[None], (8, 4, 128)), 'tomo', split_ax...]
  transfers between devices with their start and end apart: 1 -> 2, of which waited for: 0 -> 2; matrix products, arithmetic and copies ran while one was open for 1% -> 1% of each run, Pallas kernels for 0% -> 0%
where the time goes in v1:
time: 120 us; the launch traced here: 119 us
  Pallas kernels  55.6 us (46%)
  blocking collectives  25.8 us (22%)
  waiting for transfers between devices  15.9 us (13%)
  starting transfers between devices  13.9 us (12%)
  local copies, waits for them, and re-layouts  6.16 us (5%)
  between operations  2 us (2%)
    pallas_call x1, Pallas kernels, work(): pl.pallas_call(work_kernel, out_shape=jax.ShapeDtypeStruct((NT, 4, 128),...  49.2 us
    all_to_all x1, blocking collectives, on_device(): lax.all_to_all(jnp.broadcast_to(own[None], (8, 4, 128)), 'tomo', split_ax...  14.6 us
    all_to_all x1, blocking collectives, on_device(): lax.all_to_all(partial, 'tilt', split_axis=0, concat_axis=0, tiled=True)  11.2 us
    all_to_all x1, waiting for transfers between devices, on_device(): lax.all_to_all(payload, 'tilt', split_axis=0, concat_axis=0, tiled=True)  8.95 us
    all_to_all x1, starting transfers between devices, on_device(): lax.all_to_all(payload, 'tilt', split_axis=0, concat_axis=0, tiled=True)  8.59 us
    all_to_all x1, waiting for transfers between devices, on_device(): lax.all_to_all(jnp.broadcast_to(chunk[None], (NT, 4, 128)), 'tilt', split...  6.92 us
    pallas_call x1, Pallas kernels, cut(): pl.pallas_call(cut_kernel, out_shape=jax.ShapeDtypeStruct((NP, 40, 128),...  6.37 us
    all_to_all x1, starting transfers between devices, on_device(): lax.all_to_all(jnp.broadcast_to(chunk[None], (NT, 4, 128)), 'tilt', split...  5.33 us
  transfers between devices with their start and end apart: 2, of which 2 were waited for; matrix products, arithmetic and copies ran while one was open for 1% of the time, Pallas kernels for 0%

profile of v1, /device:TPU:1, one launch (start us, length us, event | category | flops | bytes accessed | tf_op | source)
XLA Modules:
  0.0 119.5 jit_solution(9890487415284659579)
XLA Ops:
  0.6 0.0 copy-start.3
  0.6 0.8 copy.25.anchor
  2.7 0.0 copy-start
  2.7 1.6 %copy-done = bf16[1,1,1024,1024]{3,2,1,0:T(8,128)(2,1)S(1)} copy-done((bf16[1,1,1024,1024]{3,2,1,0:T(8,128)(2,1)S(1)}, bf16[1,1,1024,1024]{3,2,1,0:T(8,128)(2,1)}, u32[]{:S(2)}) %copy-start) | copy-done | bytes 2097176
  4.3 0.0 copy-start.1
  4.3 0.7 copy-done.1
  5.0 6.4 %shard_map.140 = bf16[32,40,128]{2,1,0:T(8,128)(2,1)} custom-call(s32[1,1,32,2]{3,2,1,0:T(8,128)S(1)} %copy.25.anchor, f32[1,1]{1,0:T(1,128)S(6)} %copy.33.angle, f32[1,1]{1,0:T(1,128)S(6)} %copy.34.focus, f32[1,1,6]{2,1,0:T(1,128)S(1)} %copy-done.1, bf16[1,1,1024,1024]{3,2,1,0:T(8,128)(2,1)S(1)} %copy-done), custom_call_target="tpu_custom_call" | custom-call | tf_op jit(solution)/shard_map/pallas_call | solution.py:127
  11.3 8.6 %all-to-all-start = ((bf16[32,40,128]{2,1,0:T(8,128)(2,1)}), bf16[32,40,128]{2,1,0:T(8,128)(2,1)S(1)}, u32[]{:S(2)}, u32[]{:S(2)}) async-start(bf16[32,40,128]{2,1,0:T(8,128)(2,1)} %shard_map.140), calls=%async_computation | async-start | bytes 655360 | tf_op jit(solution)/shard_map/all_to_all | solution.py:459
  19.9 0.0 copy-done.3
  19.9 0.6 copy.26.euler
  20.5 8.9 %all-to-all-done.received = bf16[32,40,128]{2,1,0:T(8,128)(2,1)S(1)} async-done(((bf16[32,40,128]{2,1,0:T(8,128)(2,1)}), bf16[32,40,128]{2,1,0:T(8,128)(2,1)S(1)}, u32[]{:S(2)}, u32[]{:S(2)}) %all-to-all-start) | async-done | bytes 327712 | tf_op jit(solution)/shard_map/all_to_all | solution.py:459
  29.5 0.0 copy-start.2
  29.5 0.7 copy-done.2
  30.2 49.2 %shard_map.141 = f32[32,4,128]{2,1,0:T(4,128)} custom-call(s32[1]{0:T(128)} %bitcast.slot, f32[1,3,32]{2,1,0:T(4,128)} %copy.26.euler, bf16[32,40,128]{2,1,0:T(8,128)(2,1)} %copy-done.2, f32[3,2048]{1,0:T(4,128)} %centers.1, f32[1,2048]{1,0:T(1,128)} %bitcast.19, f32[1,2048]{1,0:T(1,128)} %bitcast.20, bf16[128,256]{1,0:T(8,128)(2,1)} %constant.14.clone.right_hi, ...), custom_call_target="tpu_custom_call" | custom-call | tf_op jit(solution)/shard_map/pallas_call | solution.py:424
  79.4 11.2 %all_to_all.20 = f32[32,4,128]{2,1,0:T(4,128)S(1)} all-to-all(f32[32,4,128]{2,1,0:T(4,128)} %shard_map.141), channel_id=1, replica_groups=mesh['tomo'=8,'tilt'=32] {'tilt'}, dimensions={0} | all-to-all | bytes 131072 | tf_op jit(solution)/shard_map/all_to_all | solution.py:462
  90.7 14.6 %all_to_all.21 = f32[8,4,128]{2,1,0:T(4,128)S(1)} all-to-all(f32[8,4,128]{2,1,0:T(4,128)S(1)} %broadcast_in_dim.4), channel_id=1, replica_groups=mesh['tomo'=8,'tilt'=32] {'tomo'}, dimensions={0} | all-to-all | bytes 32768 | tf_op jit(solution)/shard_map/all_to_all | solution.py:465
  105.3 0.6 broadcast_in_dim.5
  106.0 5.3 %all-to-all-start.3 = ((f32[32,4,128]{2,1,0:T(4,128)}), f32[32,4,128]{2,1,0:T(4,128)S(1)}, u32[]{:S(2)}, u32[]{:S(2)}) async-start(f32[32,4,128]{2,1,0:T(4,128)} %broadcast_in_dim.5), calls=%async_computation.3 | async-start | bytes 131072 | tf_op jit(solution)/shard_map/all_to_all | solution.py:469
  111.3 0.5 slice_bitcast_fusion
  111.8 6.9 %all-to-all-done.3 = f32[32,4,128]{2,1,0:T(4,128)S(1)} async-done(((f32[32,4,128]{2,1,0:T(4,128)}), f32[32,4,128]{2,1,0:T(4,128)S(1)}, u32[]{:S(2)}, u32[]{:S(2)}) %all-to-all-start.3) | async-done | bytes 65568 | tf_op jit(solution)/shard_map/all_to_all | solution.py:469
  118.8 0.6 copy.32
  (7 shorter events, 0.1 us)
Async XLA Ops:
  0.6 19.3 %copy-start.3 = (f32[1,3,32]{2,0,1:T(1,128)S(1)}, f32[1,3,32]{2,0,1:T(1,128)}, u32[]{:S(2)}) copy-start(f32[1,3,32]{2,0,1:T(1,128)} %param.15) | copy-start | bytes 1156
  2.7 1.6 %copy-start = (bf16[1,1,1024,1024]{3,2,1,0:T(8,128)(2,1)S(1)}, bf16[1,1,1024,1024]{3,2,1,0:T(8,128)(2,1)}, u32[]{:S(2)}) copy-start(bf16[1,1,1024,1024]{3,2,1,0:T(8,128)(2,1)} %image.1) | copy-start | bytes 6291460
  4.3 0.7 copy-start.1
  11.3 18.1 %all-to-all-start = ((bf16[32,40,128]{2,1,0:T(8,128)(2,1)}), bf16[32,40,128]{2,1,0:T(8,128)(2,1)S(1)}, u32[]{:S(2)}, u32[]{:S(2)}) async-start(bf16[32,40,128]{2,1,0:T(8,128)(2,1)} %shard_map.140), calls=%async_computation | async-start | bytes 655360 | tf_op jit(solution)/shard_map/all_to_all | solution.py:459
  29.5 0.7 copy-start.2
  106.0 12.8 %all-to-all-start.3 = ((f32[32,4,128]{2,1,0:T(4,128)}), f32[32,4,128]{2,1,0:T(4,128)S(1)}, u32[]{:S(2)}, u32[]{:S(2)}) async-start(f32[32,4,128]{2,1,0:T(4,128)} %broadcast_in_dim.5), calls=%async_computation.3 | async-start | bytes 131072 | tf_op jit(solution)/shard_map/all_to_all | solution.py:469

commit v2 on v1

v2 whole, which is shorter than its diff:
```python
import math

import jax
import jax.numpy as jnp
import numpy as np
from jax import lax
from jax.experimental import pallas as pl
from jax.experimental.pallas import tpu as pltpu
from jax.sharding import PartitionSpec as P

G = 2048
BOX = 64
IMG = 1024
NT = 32
NP = 32
CH = 256
NCH = G // CH
HALF = 40
ROWS = 2 * HALF
UF, US, UR, UB = 2, 8, 8, 2
F32 = jnp.float32
BF16 = jnp.bfloat16


def _fit(fn, degree):
    n = 64
    nodes = 0.125 * (1 + np.cos(np.pi * (np.arange(n) + 0.5) / n))
    return [float(c) for c in np.polynomial.polynomial.polyfit(nodes, fn(np.sqrt(nodes)), degree)]


SIN_POLY = _fit(lambda u: np.sin(np.pi * u) / u, 5)
COS_POLY = _fit(lambda u: np.cos(np.pi * u), 5)


def _horner(w, coefs):
    acc = jnp.full_like(w, coefs[-1])
    for c in coefs[-2::-1]:
        acc = acc * w + c
    return acc


def cos_sin_turns(turns):
    u = turns - jnp.round(turns)
    w = u * u
    s = u * _horner(w, SIN_POLY)
    c = _horner(w, COS_POLY)
    return 1.0 - 2.0 * (s * s), 2.0 * (s * c)


def split(x):
    hi = x.astype(BF16)
    return hi, (x - hi.astype(F32)).astype(BF16)


def np_split(x):
    hi = x.astype(jnp.bfloat16)
    lo = (x - hi.astype(np.float64)).astype(jnp.bfloat16)
    return hi, lo


def tables():
    pos = np.arange(BOX)
    freq = np.arange(33)
    ang = 2 * np.pi * ((pos[:, None] * freq[None, :]) % BOX) / BOX
    lanes = np.zeros((BOX, 128))
    lanes[:, :33] = np.cos(ang)
    lanes[:, 64:97] = np.sin(ang)
    right = np.zeros((128, 256))
    right[:64, :128] = lanes
    right[64:, 128:] = lanes
    right_hi, right_lo = np_split(right)
    rows = np.zeros((ROWS, BOX))
    rows[:33] = np.cos(ang).T / BOX
    rows[HALF : HALF + 33] = np.sin(ang).T / BOX
    left_hi, left_lo = np_split(rows)
    left = np.concatenate([left_hi, left_hi, left_lo], 1)
    phi = np.ones(33)
    phi[0] = phi[32] = 0.5
    both = -4.0 / (NT * NP) * phi[:, None] * phi[None, :]
    plus, minus = both.copy(), both.copy()
    plus[32, 32] *= 2.0
    minus[32, 32] = 0.0
    aux = np.zeros((3, HALF, 128), np.float32)
    for base in (0, 64):
        aux[0, :33, base : base + 33] = freq[:, None] ** 2 + freq[None, :] ** 2
        aux[1, :33, base : base + 33] = plus
        aux[2, :33, base : base + 33] = minus
    joiner = np.zeros((256, 2 * ROWS), jnp.bfloat16)
    chooser = np.zeros((ROWS, 128), jnp.bfloat16)
    for i in range(HALF):
        for part in (0, 1):
            joiner[128 * part + i, ROWS * part + i] = 1
            joiner[128 * part + 64 + i, ROWS * part + HALF + i] = 1
        chooser[i, i] = 1
        chooser[HALF + i, 64 + i] = 1
    return right_hi, right_lo, left, joiner, chooser, aux


def cut_kernel(anchor, angle, focus, warp, image, out, windows, sem, strip):
    def source(p):
        r, c = anchor[0, 0, 0, p], anchor[0, 0, 1, p]
        r0 = pl.multiple_of(jnp.minimum((r // 16) * 16, IMG - 80), 16)
        c0 = pl.multiple_of(jnp.minimum((c // 128) * 128, IMG - 256), 128)
        return r, c, r0, c0

    def copy(p):
        _, _, r0, c0 = source(p)
        return pltpu.make_async_copy(
            image.at[0, 0, pl.ds(r0, 80), pl.ds(c0, 256)], windows.at[p], sem.at[p]
        )

    def start(p, carry):
        copy(p).start()
        return carry

    lax.fori_loop(0, NP, start, 0, unroll=4)

    lane = lax.broadcasted_iota(jnp.int32, (8, 128), 1)
    sub = lax.broadcasted_iota(jnp.int32, (8, 128), 0)
    values = [angle[0, 0], focus[0, 0]] + [warp[0, 0, i] for i in range(6)]
    row = jnp.zeros((8, 128), F32)
    for i, v in enumerate(values):
        row = jnp.where(lane == i, v, row)
    hi = row.astype(BF16).astype(F32)
    mid = (row - hi).astype(BF16).astype(F32)
    low = row - hi - mid
    parts = jnp.where(sub == 0, hi, jnp.where(sub == 1, mid, jnp.where(sub == 2, low, 0.0)))
    left_half = lax.broadcasted_iota(jnp.int32, (32, 128), 1) < BOX

    def one(p, carry):
        copy(p).wait()
        r, c, r0, c0 = source(p)
        turned = pltpu.roll(windows[p].astype(F32), 256 - (c - c0), 1)[:, :128]
        strip[p % 8] = turned
        upper = strip[p % 8, pl.ds(r - r0, 32), :]
        lower = strip[p % 8, pl.ds(r - r0 + 32, 32), :]
        packed = jnp.where(left_half, upper, pltpu.roll(lower, 64, 1))
        out[p] = jnp.concatenate([packed, parts], 0).astype(BF16)
        return carry

    lax.fori_loop(0, NP, one, 0, unroll=8)


def cut(images, anchors, angle, focus, warp):
    smem = pl.BlockSpec(memory_space=pltpu.SMEM)
    return pl.pallas_call(
        cut_kernel,
        out_shape=jax.ShapeDtypeStruct((NP, 40, 128), BF16),
        in_specs=[smem, smem, smem, smem, pl.BlockSpec(memory_space=pl.ANY)],
        out_specs=pl.BlockSpec(memory_space=pltpu.VMEM),
        scratch_shapes=[
            pltpu.VMEM((NP, 80, 256), BF16),
            pltpu.SemaphoreType.DMA((NP,)),
            pltpu.VMEM((8, 80, 128), F32),
        ],
        compiler_params=pltpu.CompilerParams(vmem_limit_bytes=55 << 20),
    )(jnp.transpose(anchors, (0, 1, 3, 2)), angle, focus, warp, images)


def work_kernel(
    slot,
    euler,
    received,
    centers,
    amplitudes,
    widths,
    right_hi,
    right_lo,
    left,
    joiner,
    chooser,
    aux,
    keep,
    send,
    xs,
    base,
    step,
    nyq,
    nyqk,
    env,
    acc,
    model,
    spectra,
    mats,
    zsc,
    focus,
    out,
):
    prm = jnp.sum(received[:, 32:40, :].astype(F32), axis=1)
    focus[...] = jnp.broadcast_to(prm[:, 1:2], (NT, 128))
    ct, st = cos_sin_turns(prm * (0.5 / math.pi))
    ct, st = ct[:, 0:1], st[:, 0:1]
    a00, a01 = 1.0 + prm[:, 2:3], prm[:, 3:4]
    a10, a11 = prm[:, 4:5], 1.0 + prm[:, 5:6]
    sh_x, sh_y = 20.0 * prm[:, 6:7], 20.0 * prm[:, 7:8]
    mine = slot[0]
    turn = []
    for i in range(3):
        angle = jnp.full((8, 128), euler[i, 0, mine], F32)
        c, s = cos_sin_turns(angle * (0.5 / math.pi))
        turn.append((c[0:1, 0:1], s[0:1, 0:1]))
    (ca, sa), (cb, sb), (cc, sc) = turn

    def rotated(sl):
        x, y, z = centers[0:1, sl], centers[1:2, sl], centers[2:3, sl]
        x, y = cc * x - sc * y, sc * x + cc * y
        x, z = cb * x + sb * z, cb * z - sb * x
        x, y = ca * x - sa * y, sa * x + ca * y
        return x, y, z

    blur = 2.0 * math.pi**2 / BOX**2
    freq8 = lax.broadcasted_iota(jnp.int32, (8, CH), 0).astype(F32)
    freq32 = lax.broadcasted_iota(jnp.int32, (32, CH), 0).astype(F32)
    first = lax.broadcasted_iota(jnp.int32, (8, CH), 0) == 0

    def prepare(c, carry):
        sl = pl.ds(pl.multiple_of(c * CH, CH), CH)
        r0, r1, r2 = rotated(sl)
        px = ct * r0 + st * r2
        ux = (a00 * px + a01 * r1 + sh_x) * (1.0 / BOX) + 0.5
        uy = (a10 * px + a11 * r1 + sh_y) * (1.0 / BOX) + 0.5
        wide = -blur * widths[0:1, sl] * widths[0:1, sl]
        damp = jnp.exp(wide * (freq32 * freq32))
        env[0, :, sl] = damp
        env[1, :, sl] = amplitudes[0:1, sl] * damp
        damp32 = jnp.exp(wide * 1024.0)
        for axis, u in ((0, ux), (1, uy)):
            u = u - jnp.round(u)
            c1, s1 = cos_sin_turns(u)
            def twice(p):
                return 1.0 - 2.0 * (p[1] * p[1]), 2.0 * (p[0] * p[1])

            def times(p, q):
                return p[0] * q[0] - p[1] * q[1], p[0] * q[1] + p[1] * q[0]

            e1 = (c1, s1)
            e2 = twice(e1)
            e3 = times(e2, e1)
            e4 = twice(e2)
            e5 = times(e4, e1)
            e6 = twice(e3)
            e7 = times(e4, e3)
            c8, s8 = e8 = twice(e4)
            cn, sn = twice(twice(e8))
            d32 = damp32 if axis == 0 else amplitudes[0:1, sl] * damp32
            nyq[2 * axis, :, sl] = cn * d32
            nyq[2 * axis + 1, :, sl] = sn * d32
            step[2 * axis, :, sl] = c8
            step[2 * axis + 1, :, sl] = s8
            e0 = (jnp.ones_like(c1), jnp.zeros_like(c1))
            for j, e in enumerate((e0, e1, e2, e3, e4, e5, e6, e7)):
                for i in range(CH // 128):
                    tile = c * (CH // 128) + i
                    lanes = slice(i * 128, i * 128 + 128)
                    base[2 * axis, tile, pl.ds(j, NT, stride=8), :] = e[0][:, lanes]
                    base[2 * axis + 1, tile, pl.ds(j, NT, stride=8), :] = e[1][:, lanes]
        return carry

    lax.fori_loop(0, NCH, prepare, 0)

    blank = jnp.zeros((24, CH), F32)

    def factors(k, axis, c):
        sl = slice(c * CH, (c + 1) * CH)
        k8 = pl.multiple_of(k * 8, 8)
        tiles = range(c * (CH // 128), (c + 1) * (CH // 128))
        gc = jnp.concatenate([base[2 * axis, t, pl.ds(k8, 8), :] for t in tiles], 1)
        gs = jnp.concatenate([base[2 * axis + 1, t, pl.ds(k8, 8), :] for t in tiles], 1)
        rc = step[2 * axis, pl.ds(k, 1), sl]
        rs = step[2 * axis + 1, pl.ds(k, 1), sl]
        cs, ss = [], []
        for m in range(4):
            damp = env[axis, 8 * m : 8 * m + 8, sl]
            cm, sm = damp * gc, damp * gs
            xs[k, axis * 64 + 8 * m : axis * 64 + 8 * m + 8, sl] = cm
            xs[k, axis * 64 + 32 + 8 * m : axis * 64 + 40 + 8 * m, sl] = sm
            cs.append(cm)
            ss.append(sm)
            if m < 3:
                gc, gs = gc * rc - gs * rs, gc * rs + gs * rc
        return cs, ss

    def ends_of(k, axis, sl):
        cn = jnp.where(first, nyq[2 * axis, pl.ds(k, 1), sl], 0.0)
        sn = jnp.where(first, nyq[2 * axis + 1, pl.ds(k, 1), sl], 0.0)
        return [cn], [sn]

    def forward(b, carry):
        total = jnp.zeros((2 * ROWS, 256), F32)
        for c in range(NCH):
            sl = slice(c * CH, (c + 1) * CH)
            left_rows, right_rows = [], []
            for k in (2 * b, 2 * b + 1):
                cs, ss = factors(k, 0, c)
                cn, sn = ends_of(k, 0, sl)
                left_rows += cs + cn + ss + sn
                cs, ss = factors(k, 1, c)
                cn, sn = ends_of(k, 1, sl)
                right_rows += cs + cn + [blank] + ss + sn + [blank]
            total = total + lax.dot_general(
                jnp.concatenate(left_rows, 0).astype(BF16),
                jnp.concatenate(right_rows, 0).astype(BF16),
                (((1,), (1,)), ((), ())),
                preferred_element_type=F32,
            )
        model[2 * b] = total[:ROWS, :128]
        model[2 * b + 1] = total[ROWS:, 128:]
        return carry

    lax.fori_loop(0, NT // 2, forward, 0, unroll=UF)

    for b in range(4):
        rows = received[8 * b : 8 * b + 8, 0:32, :].reshape(256, 128)
        zsc[256 * b : 256 * b + 256, :] = jnp.dot(
            rows, right_hi[...], preferred_element_type=F32
        ) + jnp.dot(rows, right_lo[...], preferred_element_type=F32)

    lane = lax.broadcasted_iota(jnp.int32, (HALF, 128), 1)
    sign = jnp.where(lane < 64, 1.0, -1.0)

    def swap(x):
        return pltpu.roll(x, 64, 1)

    def spectrum(k, sums):
        z = zsc[pl.ds(pl.multiple_of(k * 32, 32), 32), :]
        z = jnp.concatenate([z[:, :128], z[:, 128:]], 0)
        z_hi, z_lo = split(z)
        p = jnp.dot(left[...], jnp.concatenate([z_hi, z_lo, z_hi], 0), preferred_element_type=F32)
        pc, ps = p[:HALF], swap(p[HALF:])
        spectra[k, :HALF] = pc
        spectra[k, HALF:] = ps
        plus, minus = sign * pc - ps, pc + sign * ps
        return sums[0] + plus * plus, sums[1] + minus * minus

    nought = jnp.zeros((HALF, 128), F32)
    plus, minus = lax.fori_loop(0, NT, spectrum, (nought, nought), unroll=US)
    f_plus = aux[1] / (0.25 + (plus + swap(plus)) * (1.0 / NT))
    f_minus = aux[2] / (0.25 + (minus + swap(minus)) * (1.0 / NT))
    radius = aux[0]

    def residual(k, carry):
        x = focus[pl.ds(k, 1), :] * radius * (1.0 / BOX) + 0.1
        n = jnp.round(x * (0.5 / math.pi))
        r = (x - n * 6.28125) - n * (2.0 * math.pi - 6.28125)
        ctf = -cos_sin_turns(r * (0.5 / math.pi))[1]
        dc = spectra[k, :HALF] - ctf * model[k, :HALF]
        ds = spectra[k, HALF:] - ctf * swap(model[k, HALF:])
        hp = (f_plus * ctf) * (sign * dc - ds)
        hm = (f_minus * ctf) * (dc + sign * ds)
        m1 = jnp.concatenate([hm, swap(sign * hm)], 0).astype(BF16)
        m2 = jnp.concatenate([sign * hp, -swap(hp)], 0).astype(BF16)
        mats[k, 0] = jnp.dot(
            jnp.concatenate([m1, m2], 1), joiner[...], preferred_element_type=F32
        ).astype(BF16)
        mats[k, 1] = lax.dot_general(
            chooser[...],
            jnp.concatenate([m1, m2], 0),
            (((1,), (1,)), ((), ())),
            preferred_element_type=F32,
        ).astype(BF16)
        return carry

    lax.fori_loop(0, NT, residual, 0, unroll=UR)

    acc[...] = jnp.zeros_like(acc)
    w1 = [freq8 + float(8 * m) for m in range(4)]
    w2 = [w * w for w in w1]

    def backward(k, carry):
        k8 = pl.multiple_of(k * 8, 8)
        for c in range(NCH):
            sl = slice(c * CH, (c + 1) * CH)
            sides, parts = [], []
            for axis in (0, 1):
                cs = [xs[k, axis * 64 + 8 * m : axis * 64 + 8 * m + 8, sl] for m in range(4)]
                ss = [xs[k, axis * 64 + 32 + 8 * m : axis * 64 + 40 + 8 * m, sl] for m in range(4)]
                cn, sn = ends_of(k, axis, sl)
                parts.append((cs, ss))
                sides.append(jnp.concatenate(cs + cn + ss + sn, 0).astype(BF16))
            backs = [
                jnp.dot(
                    mats[k, axis],
                    jnp.concatenate([sides[1 - axis]] * 2, 0),
                    preferred_element_type=F32,
                )
                for axis in (0, 1)
            ]
            width_sum = acc[0, :, sl]
            value_sum = acc[1, :, sl]
            moves = [None, None]
            for m in range(4):
                values = []
                for axis in (0, 1):
                    c_m, s_m = parts[axis][0][m], parts[axis][1][m]
                    kc = backs[axis][8 * m : 8 * m + 8]
                    ks = backs[axis][HALF + 8 * m : HALF + 8 * m + 8]
                    values.append(c_m * kc + s_m * ks)
                    move = w1[m] * (c_m * ks - s_m * kc)
                    moves[axis] = move if m == 0 else moves[axis] + move
                value_sum = value_sum + values[1]
                width_sum = width_sum + w2[m] * (values[0] + values[1])
            acc[0, :, sl] = width_sum
            acc[1, :, sl] = value_sum
            for axis in (0, 1):
                for i in range(CH // 128):
                    lanes = slice(i * 128, i * 128 + 128)
                    base[axis, c * (CH // 128) + i, pl.ds(k8, 8), :] = moves[axis][:, lanes]
                nyqk[2 * axis, pl.ds(k, 1), sl] = backs[axis][32:33]
                nyqk[2 * axis + 1, pl.ds(k, 1), sl] = backs[axis][HALF + 32 : HALF + 33]
        return carry

    lax.fori_loop(0, NT, backward, 0, unroll=UB)

    terms = [jnp.zeros((NT, 128), F32) for _ in range(6)]
    unit = 2.0 * math.pi / BOX
    for c in range(G // 128):
        sl = slice(c * 128, (c + 1) * 128)
        moves, ends = [], []
        for axis in (0, 1):
            move = base[axis, c, pl.ds(0, NT, stride=8), :]
            for j in range(1, 8):
                move = move + base[axis, c, pl.ds(j, NT, stride=8), :]
            nc, ns = nyq[2 * axis, :, sl], nyq[2 * axis + 1, :, sl]
            kc, ks = nyqk[2 * axis, :, sl], nyqk[2 * axis + 1, :, sl]
            moves.append(unit * (move + 32.0 * (nc * ks - ns * kc)))
            ends.append(jnp.sum(nc * kc + ns * ks, axis=0, keepdims=True))
        mx, my = moves
        r0, r1, r2 = rotated(sl)
        px = ct * r0 + st * r2
        for i, t in enumerate((mx * px, mx * r1, my * px, my * r1, mx, my)):
            terms[i] = terms[i] + t
        vx = a00 * mx + a10 * my
        vy = a01 * mx + a11 * my
        x = jnp.sum(ct * vx, axis=0, keepdims=True)
        z = jnp.sum(st * vx, axis=0, keepdims=True)
        y = jnp.sum(vy, axis=0, keepdims=True)
        x, y = ca * x + sa * y, ca * y - sa * x
        x, z = cb * x - sb * z, sb * x + cb * z
        x, y = cc * x + sc * y, cc * y - sc * x
        curve = jnp.sum(acc[0, :, sl], axis=0, keepdims=True) + 1024.0 * (ends[0] + ends[1])
        value = jnp.sum(acc[1, :, sl], axis=0, keepdims=True) + ends[1]
        half, lanes = c // 8, slice((c % 8) * 128, (c % 8) * 128 + 128)
        out[half, 0:1, lanes] = x
        out[half, 1:2, lanes] = y
        out[half, 2:3, lanes] = z
        out[half, 3:4, lanes] = value / amplitudes[0:1, sl]
        out[half, 4:5, lanes] = (-2.0 * blur) * widths[0:1, sl] * curve
    lane_w = lax.broadcasted_iota(jnp.int32, (NT, 128), 1)
    warp_rows = jnp.zeros((NT, 128), F32)
    for i in range(6):
        total = jnp.sum(terms[i], axis=1, keepdims=True) * (20.0 if i > 3 else 1.0)
        warp_rows = jnp.where(lane_w == i, total, warp_rows)
    for k in range(NT):
        i = k // 2
        out[k % 2, 5 + i // 8 : 6 + i // 8, (i % 8) * 128 : (i % 8) * 128 + 128] = warp_rows[k : k + 1]
    core = mine % 2
    keep[...] = out[core]
    send[...] = out[1 - core]


def work(slot, euler, received, centers, amplitudes, widths):
    smem = pl.BlockSpec(memory_space=pltpu.SMEM)
    vmem = pl.BlockSpec(memory_space=pltpu.VMEM)
    right_hi, right_lo, left, joiner, chooser, aux = tables()
    return pl.pallas_call(
        work_kernel,
        out_shape=[jax.ShapeDtypeStruct((8, G // 2), F32)] * 2,
        in_specs=[smem, smem] + [vmem] * 10,
        out_specs=[vmem, vmem],
        scratch_shapes=[
            pltpu.VMEM((NT, 128, G), F32),
            pltpu.VMEM((4, G // 128, NT * 8, 128), F32),
            pltpu.VMEM((4, NT, G), F32),
            pltpu.VMEM((4, NT, G), F32),
            pltpu.VMEM((4, NT, G), F32),
            pltpu.VMEM((2, 32, G), F32),
            pltpu.VMEM((2, 8, G), F32),
            pltpu.VMEM((NT, ROWS, 128), F32),
            pltpu.VMEM((NT, ROWS, 128), F32),
            pltpu.VMEM((NT, 2, ROWS, 2 * ROWS), BF16),
            pltpu.VMEM((1024, 256), F32),
            pltpu.VMEM((NT, 128), F32),
            pltpu.VMEM((2, 8, G // 2), F32),
        ],
        compiler_params=pltpu.CompilerParams(vmem_limit_bytes=55 << 20),
    )(
        slot,
        jnp.transpose(euler, (1, 0, 2)),
        received,
        centers,
        amplitudes.reshape(1, G),
        widths.reshape(1, G),
        jnp.asarray(right_hi),
        jnp.asarray(right_lo),
        jnp.asarray(left),
        jnp.asarray(joiner),
        jnp.asarray(chooser),
        jnp.asarray(aux),
    )


def exchanged(value, axis, mask):
    return lax.ppermute(value, axis, [(i, i ^ mask) for i in range(lax.axis_size(axis))])


def on_device(tilt_images, anchors, euler, tilt_angle, defocus, warp, centers, amplitudes, widths):
    payload = cut(tilt_images, anchors, tilt_angle, defocus, warp)
    received = lax.all_to_all(payload, "tilt", split_axis=0, concat_axis=0, tiled=True)
    index = lax.axis_index("tilt").astype(jnp.int32)
    total, other = work(index.reshape(1), euler, received, centers, amplitudes, widths)
    total = total + exchanged(other, "tilt", 1)
    for mask in (2, 6, 8, 24):
        total = total + exchanged(total, "tilt", mask)
    place = index // 2
    warp_local = lax.dynamic_slice(total, (5 + place // 8, (place % 8) * 128), (1, 6))
    for mask in (1, 2, 7):
        total = total + exchanged(total, "tomo", mask)
    other = exchanged(total, "tilt", 1)
    first = index % 2 == 0
    template = jnp.concatenate(
        [jnp.where(first, total, other)[:5], jnp.where(first, other, total)[:5]], 1
    )
    return (template, warp_local.reshape(1, 1, 6))


def solution(mesh):
    placed = (
        P("tomo", "tilt", None, None),
        P("tomo", "tilt", None, None),
        P("tomo", None, None),
        P("tomo", "tilt"),
        P("tomo", "tilt"),
        P("tomo", "tilt", None),
        P(),
        P(),
        P(),
    )
    return jax.shard_map(
        on_device,
        mesh=mesh,
        in_specs=placed,
        out_specs=(P(), P("tomo", "tilt", None)),
        check_vma=False,
    )
```

time: 120 us -> 98.5 us (0.82)
  blocking collectives: 25.8 us -> 0 us
  Pallas kernels: 55.6 us -> 38.8 us
  starting transfers between devices: 13.9 us -> 29.2 us
  waiting for transfers between devices: 15.9 us -> 25.5 us
  local copies, waits for them, and re-layouts: 6.16 us -> 1.3 us
  other arithmetic: 0.07 us -> 1.45 us
    all_to_all x2 -> x0, blocking collectives: 25.8 us -> none  [the longest x1 14.6 us: on_device(): lax.all_to_all(jnp.broadcast_to(own[None], (8, 4, 128)), 'tomo', split_ax...]
    ppermute x0 -> x9, starting transfers between devices: none -> 20.6 us  [exchanged(): lax.ppermute(value, axis, [(i, i ^ mask) for i in range(lax.axis_size(axi...]
    pallas_call x1, Pallas kernels: 49.2 us -> 31.1 us  [work(): pl.pallas_call(work_kernel, out_shape=[jax.ShapeDtypeStruct((8, G // 2),...]
    ppermute x0 -> x9, waiting for transfers between devices: none -> 16 us  [exchanged(): lax.ppermute(value, axis, [(i, i ^ mask) for i in range(lax.axis_size(axi...]
    all_to_all x1 -> x0, waiting for transfers between devices: 6.92 us -> none  [on_device(): lax.all_to_all(jnp.broadcast_to(chunk[None], (NT, 4, 128)), 'tilt', split...]
    all_to_all x1 -> x0, starting transfers between devices: 5.33 us -> none  [on_device(): lax.all_to_all(jnp.broadcast_to(chunk[None], (NT, 4, 128)), 'tilt', split...]
    unnamed x11 -> x2, local copies, waits for them, and re-layouts: 4.95 us -> 0.71 us
    pallas_call x1, Pallas kernels: 6.37 us -> 7.71 us  [cut(): pl.pallas_call(cut_kernel, out_shape=jax.ShapeDtypeStruct((NP, 40, 128),...]
  transfers between devices with their start and end apart: 2 -> 10, of which waited for: 2 -> 10; matrix products, arithmetic and copies ran while one was open for 1% -> 1% of each run, Pallas kernels for 0% -> 0%
where the time goes in v2:
time: 98.5 us; the launch traced here: 98.2 us
  Pallas kernels  38.8 us (39%)
  starting transfers between devices  29.2 us (30%)
  waiting for transfers between devices  25.5 us (26%)
  between operations  1.96 us (2%)
  other arithmetic  1.45 us (1%)
  local copies, waits for them, and re-layouts  1.3 us (1%)
    pallas_call x1, Pallas kernels, work(): pl.pallas_call(work_kernel, out_shape=[jax.ShapeDtypeStruct((8, G // 2),...  31.1 us
    ppermute x9, starting transfers between devices, exchanged(): lax.ppermute(value, axis, [(i, i ^ mask) for i in range(lax.axis_size(axi...  20.6 us
    ppermute x9, waiting for transfers between devices, exchanged(): lax.ppermute(value, axis, [(i, i ^ mask) for i in range(lax.axis_size(axi...  16 us
    all_to_all x1, waiting for transfers between devices, on_device(): lax.all_to_all(payload, 'tilt', split_axis=0, concat_axis=0, tiled=True)  9.53 us
    all_to_all x1, starting transfers between devices, on_device(): lax.all_to_all(payload, 'tilt', split_axis=0, concat_axis=0, tiled=True)  8.6 us
    pallas_call x1, Pallas kernels, cut(): pl.pallas_call(cut_kernel, out_shape=jax.ShapeDtypeStruct((NP, 40, 128),...  7.71 us
  transfers between devices with their start and end apart: 10, of which 10 were waited for; matrix products, arithmetic and copies ran while one was open for 1% of the time, Pallas kernels for 0%

profile of v2, /device:TPU:1, one launch (start us, length us, event | category | flops | bytes accessed | tf_op | source)
XLA Modules:
  0.0 98.2 jit_solution(1971565283150661756)
XLA Ops:
  1.9 7.7 %shard_map.158 = bf16[32,40,128]{2,1,0:T(8,128)(2,1)} custom-call(s32[1,1,2,32]{3,2,1,0:T(2,128)} %bitcast.10, f32[1,1]{1,0:T(1,128)S(6)} %copy.17.angle, f32[1,1]{1,0:T(1,128)S(6)} %copy.18.focus, f32[1,1,6]{2,1,0:T(1,128)} %warp.1, bf16[1,1,1024,1024]{3,2,1,0:T(8,128)(2,1)} %image.1), custom_call_target="tpu_custom_call" | custom-call | tf_op jit(solution)/shard_map/pallas_call | solution.py:146
  9.6 8.6 %all-to-all-start = ((bf16[32,40,128]{2,1,0:T(8,128)(2,1)}), bf16[32,40,128]{2,1,0:T(8,128)(2,1)S(1)}, u32[]{:S(2)}, u32[]{:S(2)}) async-start(bf16[32,40,128]{2,1,0:T(8,128)(2,1)} %shard_map.158), calls=%async_computation | async-start | bytes 655360 | tf_op jit(solution)/shard_map/all_to_all | solution.py:508
  18.2 9.5 %all-to-all-done.received = bf16[32,40,128]{2,1,0:T(8,128)(2,1)S(1)} async-done(((bf16[32,40,128]{2,1,0:T(8,128)(2,1)}), bf16[32,40,128]{2,1,0:T(8,128)(2,1)S(1)}, u32[]{:S(2)}, u32[]{:S(2)}) %all-to-all-start) | async-done | bytes 327712 | tf_op jit(solution)/shard_map/all_to_all | solution.py:508
  27.8 0.0 copy-start
  27.8 0.7 copy-done
  28.5 31.1 %shard_map.159 = (f32[8,1024]{1,0:T(8,128)}, f32[8,1024]{1,0:T(8,128)}) custom-call(s32[1]{0:T(128)} %bitcast.slot, f32[3,1,32]{2,1,0:T(1,128)} %bitcast.9, bf16[32,40,128]{2,1,0:T(8,128)(2,1)} %copy-done, f32[3,2048]{1,0:T(4,128)} %centers.1, f32[1,2048]{1,0:T(1,128)} %bitcast.7, f32[1,2048]{1,0:T(1,128)} %bitcast.8, ...), custom_call_target="tpu_custom_call" | custom-call | tf_op jit(solution)/shard_map/pallas_call | solution.py:465
  59.6 0.3 collective-permute-start
  59.9 1.1 %collective-permute-done = f32[8,1024]{1,0:T(8,128)S(1)} collective-permute-done((f32[8,1024]{1,0:T(8,128)}, f32[8,1024]{1,0:T(8,128)S(1)}, u32[]{:S(2)}, u32[]{:S(2)}) %collective-permute-start) | collective-permute-done | bytes 32800 | tf_op jit(solution)/shard_map/ppermute | solution.py:503
  61.0 0.8 add.42
  61.8 0.5 collective-permute-start.1
  62.3 2.2 %collective-permute-done.1 = f32[8,1024]{1,0:T(8,128)S(1)} collective-permute-done((f32[8,1024]{1,0:T(8,128)S(1)}, f32[8,1024]{1,0:T(8,128)S(1)}, u32[]{:S(2)}, u32[]{:S(2)}) %collective-permute-start.1) | collective-permute-done | bytes 32800 | tf_op jit(solution)/shard_map/ppermute | solution.py:503
  64.5 1.2 %collective-permute-start.2 = (f32[8,1024]{1,0:T(8,128)S(1)}, f32[8,1024]{1,0:T(8,128)S(1)}, u32[]{:S(2)}, u32[]{:S(2)}) collective-permute-start(f32[8,1024]{1,0:T(8,128)S(1)} %add.43), channel_id=1, source_target_pairs={{0,6},{1,7},{2,4},{3,5},{4,2},{5,3},{6,0},{7,1},{8,14},{9,15},{10,... | collective-permute-start | bytes 98312 | tf_op jit(solution)/shard_map/ppermute | solution.py:503
  65.7 2.8 %collective-permute-done.2 = f32[8,1024]{1,0:T(8,128)S(1)} collective-permute-done((f32[8,1024]{1,0:T(8,128)S(1)}, f32[8,1024]{1,0:T(8,128)S(1)}, u32[]{:S(2)}, u32[]{:S(2)}) %collective-permute-start.2) | collective-permute-done | bytes 32800 | tf_op jit(solution)/shard_map/ppermute | solution.py:503
  68.5 0.3 collective-permute-start.3
  68.8 2.4 %collective-permute-done.3 = f32[8,1024]{1,0:T(8,128)S(1)} collective-permute-done((f32[8,1024]{1,0:T(8,128)S(1)}, f32[8,1024]{1,0:T(8,128)S(1)}, u32[]{:S(2)}, u32[]{:S(2)}) %collective-permute-start.3) | collective-permute-done | bytes 32800 | tf_op jit(solution)/shard_map/ppermute | solution.py:503
  71.3 0.9 collective-permute-start.4
  72.2 3.1 %collective-permute-done.4 = f32[8,1024]{1,0:T(8,128)S(1)} collective-permute-done((f32[8,1024]{1,0:T(8,128)S(1)}, f32[8,1024]{1,0:T(8,128)S(1)}, u32[]{:S(2)}, u32[]{:S(2)}) %collective-permute-start.4) | collective-permute-done | bytes 32800 | tf_op jit(solution)/shard_map/ppermute | solution.py:503
  75.3 1.6 %collective-permute-start.5 = (f32[8,1024]{1,0:T(8,128)S(1)}, f32[8,1024]{1,0:T(8,128)S(1)}, u32[]{:S(2)}, u32[]{:S(2)}) collective-permute-start(f32[8,1024]{1,0:T(8,128)S(1)} %add.46), channel_id=1, source_target_pairs={{0,32},{32,0},{64,96},{96,64},{128,160},{160,128},{192,224},{224,1... | collective-permute-start | bytes 98312 | tf_op jit(solution)/shard_map/ppermute | solution.py:503
  76.9 1.3 %collective-permute-done.5 = f32[8,1024]{1,0:T(8,128)S(1)} collective-permute-done((f32[8,1024]{1,0:T(8,128)S(1)}, f32[8,1024]{1,0:T(8,128)S(1)}, u32[]{:S(2)}, u32[]{:S(2)}) %collective-permute-start.5) | collective-permute-done | bytes 32800 | tf_op jit(solution)/shard_map/ppermute | solution.py:503
  78.2 3.0 %collective-permute-start.6 = (f32[8,1024]{1,0:T(8,128)S(1)}, f32[8,1024]{1,0:T(8,128)S(1)}, u32[]{:S(2)}, u32[]{:S(2)}) collective-permute-start(f32[8,1024]{1,0:T(8,128)S(1)} %add.47), channel_id=1, source_target_pairs={{0,64},{32,96},{64,0},{96,32},{128,192},{160,224},{192,128},{224,1... | collective-permute-start | bytes 98312 | tf_op jit(solution)/shard_map/ppermute | solution.py:503
  81.2 1.3 %collective-permute-done.6 = f32[8,1024]{1,0:T(8,128)S(1)} collective-permute-done((f32[8,1024]{1,0:T(8,128)S(1)}, f32[8,1024]{1,0:T(8,128)S(1)}, u32[]{:S(2)}, u32[]{:S(2)}) %collective-permute-start.6) | collective-permute-done | bytes 32800 | tf_op jit(solution)/shard_map/ppermute | solution.py:503
  82.5 4.8 %collective-permute-start.7 = (f32[8,1024]{1,0:T(8,128)S(1)}, f32[8,1024]{1,0:T(8,128)S(1)}, u32[]{:S(2)}, u32[]{:S(2)}) collective-permute-start(f32[8,1024]{1,0:T(8,128)S(1)} %add.48), channel_id=1, source_target_pairs={{0,224},{32,192},{64,160},{96,128},{128,96},{160,64},{192,32},{224... | collective-permute-start | bytes 98312 | tf_op jit(solution)/shard_map/ppermute | solution.py:503
  87.3 1.4 %collective-permute-done.7 = f32[8,1024]{1,0:T(8,128)S(1)} collective-permute-done((f32[8,1024]{1,0:T(8,128)S(1)}, f32[8,1024]{1,0:T(8,128)S(1)}, u32[]{:S(2)}, u32[]{:S(2)}) %collective-permute-start.7) | collective-permute-done | bytes 32800 | tf_op jit(solution)/shard_map/ppermute | solution.py:503
  88.7 7.9 %collective-permute-start.8 = (f32[8,1024]{1,0:T(8,128)S(1)}, f32[8,1024]{1,0:T(8,128)S(1)}, u32[]{:S(2)}, u32[]{:S(2)}) collective-permute-start(f32[8,1024]{1,0:T(8,128)S(1)} %add.49), channel_id=1, source_target_pairs={{0,1},{1,0},{2,3},{3,2},{4,5},{5,4},{6,7},{7,6},{8,9},{9,8},{10,11... | collective-permute-start | bytes 98312 | tf_op jit(solution)/shard_map/ppermute | solution.py:503
  96.7 0.6 dynamic-slice_bitcast_fusion
  97.2 0.3 collective-permute-done.8
  97.5 0.6 pad_maximum_fusion
  (8 shorter events, 0.0 us)
Async XLA Ops:
  9.6 18.1 %all-to-all-start = ((bf16[32,40,128]{2,1,0:T(8,128)(2,1)}), bf16[32,40,128]{2,1,0:T(8,128)(2,1)S(1)}, u32[]{:S(2)}, u32[]{:S(2)}) async-start(bf16[32,40,128]{2,1,0:T(8,128)(2,1)} %shard_map.158), calls=%async_computation | async-start | bytes 655360 | tf_op jit(solution)/shard_map/all_to_all | solution.py:508
  27.8 0.7 copy-start
  59.6 1.4 %collective-permute-start = (f32[8,1024]{1,0:T(8,128)}, f32[8,1024]{1,0:T(8,128)S(1)}, u32[]{:S(2)}, u32[]{:S(2)}) collective-permute-start(f32[8,1024]{1,0:T(8,128)} %get-tuple-element.5), channel_id=1, source_target_pairs={{0,1},{1,0},{2,3},{3,2},{4,5},{5,4},{6,7},{7,6},{8,9},{9,8},{10,11... | collective-permute-start | bytes 98312 | tf_op jit(solution)/shard_map/ppermute | solution.py:503
  61.8 2.8 %collective-permute-start.1 = (f32[8,1024]{1,0:T(8,128)S(1)}, f32[8,1024]{1,0:T(8,128)S(1)}, u32[]{:S(2)}, u32[]{:S(2)}) collective-permute-start(f32[8,1024]{1,0:T(8,128)S(1)} %add.42), channel_id=1, source_target_pairs={{0,2},{1,3},{2,0},{3,1},{4,6},{5,7},{6,4},{7,5},{8,10},{9,11},{10,... | collective-permute-start | bytes 98312 | tf_op jit(solution)/shard_map/ppermute | solution.py:503
  64.5 4.0 %collective-permute-start.2 = (f32[8,1024]{1,0:T(8,128)S(1)}, f32[8,1024]{1,0:T(8,128)S(1)}, u32[]{:S(2)}, u32[]{:S(2)}) collective-permute-start(f32[8,1024]{1,0:T(8,128)S(1)} %add.43), channel_id=1, source_target_pairs={{0,6},{1,7},{2,4},{3,5},{4,2},{5,3},{6,0},{7,1},{8,14},{9,15},{10,... | collective-permute-start | bytes 98312 | tf_op jit(solution)/shard_map/ppermute | solution.py:503
  68.5 2.8 %collective-permute-start.3 = (f32[8,1024]{1,0:T(8,128)S(1)}, f32[8,1024]{1,0:T(8,128)S(1)}, u32[]{:S(2)}, u32[]{:S(2)}) collective-permute-start(f32[8,1024]{1,0:T(8,128)S(1)} %add.44), channel_id=1, source_target_pairs={{0,8},{1,9},{2,10},{3,11},{4,12},{5,13},{6,14},{7,15},{8,0},{9,1},... | collective-permute-start | bytes 98312 | tf_op jit(solution)/shard_map/ppermute | solution.py:503
  71.3 4.0 %collective-permute-start.4 = (f32[8,1024]{1,0:T(8,128)S(1)}, f32[8,1024]{1,0:T(8,128)S(1)}, u32[]{:S(2)}, u32[]{:S(2)}) collective-permute-start(f32[8,1024]{1,0:T(8,128)S(1)} %add.45), channel_id=1, source_target_pairs={{0,24},{1,25},{2,26},{3,27},{4,28},{5,29},{6,30},{7,31},{8,16},{9,... | collective-permute-start | bytes 98312 | tf_op jit(solution)/shard_map/ppermute | solution.py:503
  75.3 2.9 %collective-permute-start.5 = (f32[8,1024]{1,0:T(8,128)S(1)}, f32[8,1024]{1,0:T(8,128)S(1)}, u32[]{:S(2)}, u32[]{:S(2)}) collective-permute-start(f32[8,1024]{1,0:T(8,128)S(1)} %add.46), channel_id=1, source_target_pairs={{0,32},{32,0},{64,96},{96,64},{128,160},{160,128},{192,224},{224,1... | collective-permute-start | bytes 98312 | tf_op jit(solution)/shard_map/ppermute | solution.py:503
  78.2 4.3 %collective-permute-start.6 = (f32[8,1024]{1,0:T(8,128)S(1)}, f32[8,1024]{1,0:T(8,128)S(1)}, u32[]{:S(2)}, u32[]{:S(2)}) collective-permute-start(f32[8,1024]{1,0:T(8,128)S(1)} %add.47), channel_id=1, source_target_pairs={{0,64},{32,96},{64,0},{96,32},{128,192},{160,224},{192,128},{224,1... | collective-permute-start | bytes 98312 | tf_op jit(solution)/shard_map/ppermute | solution.py:503
  82.5 6.2 %collective-permute-start.7 = (f32[8,1024]{1,0:T(8,128)S(1)}, f32[8,1024]{1,0:T(8,128)S(1)}, u32[]{:S(2)}, u32[]{:S(2)}) collective-permute-start(f32[8,1024]{1,0:T(8,128)S(1)} %add.48), channel_id=1, source_target_pairs={{0,224},{32,192},{64,160},{96,128},{128,96},{160,64},{192,32},{224... | collective-permute-start | bytes 98312 | tf_op jit(solution)/shard_map/ppermute | solution.py:503
  88.7 8.8 %collective-permute-start.8 = (f32[8,1024]{1,0:T(8,128)S(1)}, f32[8,1024]{1,0:T(8,128)S(1)}, u32[]{:S(2)}, u32[]{:S(2)}) collective-permute-start(f32[8,1024]{1,0:T(8,128)S(1)} %add.49), channel_id=1, source_target_pairs={{0,1},{1,0},{2,3},{3,2},{4,5},{5,4},{6,7},{7,6},{8,9},{9,8},{10,11... | collective-permute-start | bytes 98312 | tf_op jit(solution)/shard_map/ppermute | solution.py:503

commit v3 on v2

--- a/solution.py
+++ b/solution.py
@@ -96,25 +96,9 @@
     return right_hi, right_lo, left, joiner, chooser, aux
 
 
-def cut_kernel(anchor, angle, focus, warp, image, out, windows, sem, strip):
-    def source(p):
-        r, c = anchor[0, 0, 0, p], anchor[0, 0, 1, p]
-        r0 = pl.multiple_of(jnp.minimum((r // 16) * 16, IMG - 80), 16)
-        c0 = pl.multiple_of(jnp.minimum((c // 128) * 128, IMG - 256), 128)
-        return r, c, r0, c0
-
-    def copy(p):
-        _, _, r0, c0 = source(p)
-        return pltpu.make_async_copy(
-            image.at[0, 0, pl.ds(r0, 80), pl.ds(c0, 256)], windows.at[p], sem.at[p]
-        )
-
-    def start(p, carry):
-        copy(p).start()
-        return carry
-
-    lax.fori_loop(0, NP, start, 0, unroll=4)
-
+def cut_kernel(anchor, angle, focus, warp, image, out, held, sem, strip):
+    copy = pltpu.make_async_copy(image.at[0, 0], held, sem)
+    copy.start()
     lane = lax.broadcasted_iota(jnp.int32, (8, 128), 1)
     sub = lax.broadcasted_iota(jnp.int32, (8, 128), 0)
     values = [angle[0, 0], focus[0, 0]] + [warp[0, 0, i] for i in range(6)]
@@ -127,10 +111,14 @@
     parts = jnp.where(sub == 0, hi, jnp.where(sub == 1, mid, jnp.where(sub == 2, low, 0.0)))
     left_half = lax.broadcasted_iota(jnp.int32, (32, 128), 1) < BOX
 
+    copy.wait()
+
     def one(p, carry):
-        copy(p).wait()
-        r, c, r0, c0 = source(p)
-        turned = pltpu.roll(windows[p].astype(F32), 256 - (c - c0), 1)[:, :128]
+        r, c = anchor[0, 0, 0, p], anchor[0, 0, 1, p]
+        r0 = pl.multiple_of(jnp.minimum((r // 16) * 16, IMG - 80), 16)
+        c0 = pl.multiple_of(jnp.minimum((c // 128) * 128, IMG - 256), 128)
+        window = held[pl.ds(r0, 80), pl.ds(c0, 256)].astype(F32)
+        turned = pltpu.roll(window, 256 - (c - c0), 1)[:, :128]
         strip[p % 8] = turned
         upper = strip[p % 8, pl.ds(r - r0, 32), :]
         lower = strip[p % 8, pl.ds(r - r0 + 32, 32), :]
@@ -149,8 +137,8 @@
         in_specs=[smem, smem, smem, smem, pl.BlockSpec(memory_space=pl.ANY)],
         out_specs=pl.BlockSpec(memory_space=pltpu.VMEM),
         scratch_shapes=[
-            pltpu.VMEM((NP, 80, 256), BF16),
-            pltpu.SemaphoreType.DMA((NP,)),
+            pltpu.VMEM((IMG, IMG), BF16),
+            pltpu.SemaphoreType.DMA,
             pltpu.VMEM((8, 80, 128), F32),
         ],
         compiler_params=pltpu.CompilerParams(vmem_limit_bytes=55 << 20),
@@ -160,7 +148,7 @@
 def work_kernel(
     slot,
     euler,
-    received,
+    incoming,
     centers,
     amplitudes,
     widths,
@@ -184,15 +172,22 @@
     mats,
     zsc,
     focus,
+    cols,
     out,
+    received,
+    sem,
 ):
+    copy = pltpu.make_async_copy(incoming, received, sem)
+    copy.start()
+    copy.wait()
     prm = jnp.sum(received[:, 32:40, :].astype(F32), axis=1)
     focus[...] = jnp.broadcast_to(prm[:, 1:2], (NT, 128))
     ct, st = cos_sin_turns(prm * (0.5 / math.pi))
-    ct, st = ct[:, 0:1], st[:, 0:1]
-    a00, a01 = 1.0 + prm[:, 2:3], prm[:, 3:4]
-    a10, a11 = prm[:, 4:5], 1.0 + prm[:, 5:6]
-    sh_x, sh_y = 20.0 * prm[:, 6:7], 20.0 * prm[:, 7:8]
+    firsts = (ct[:, 0:1], st[:, 0:1])
+    rest = (1.0 + prm[:, 2:3], prm[:, 3:4], prm[:, 4:5], 1.0 + prm[:, 5:6])
+    shifts = (20.0 * prm[:, 6:7], 20.0 * prm[:, 7:8])
+    for i, column in enumerate(firsts + rest + shifts):
+        cols[i] = jnp.broadcast_to(column, (NT, 128))
     mine = slot[0]
     turn = []
     for i in range(3):
@@ -216,6 +211,9 @@
     def prepare(c, carry):
         sl = pl.ds(pl.multiple_of(c * CH, CH), CH)
         r0, r1, r2 = rotated(sl)
+        ct, st, a00, a01, a10, a11, sh_x, sh_y = (
+            jnp.concatenate([cols[i]] * (CH // 128), 1) for i in range(8)
+        )
         px = ct * r0 + st * r2
         ux = (a00 * px + a01 * r1 + sh_x) * (1.0 / BOX) + 0.5
         uy = (a10 * px + a11 * r1 + sh_y) * (1.0 / BOX) + 0.5
@@ -413,6 +411,7 @@
 
     terms = [jnp.zeros((NT, 128), F32) for _ in range(6)]
     unit = 2.0 * math.pi / BOX
+    ct, st, a00, a01, a10, a11 = (cols[i] for i in range(6))
     for c in range(G // 128):
         sl = slice(c * 128, (c + 1) * 128)
         moves, ends = [], []
@@ -465,7 +464,7 @@
     return pl.pallas_call(
         work_kernel,
         out_shape=[jax.ShapeDtypeStruct((8, G // 2), F32)] * 2,
-        in_specs=[smem, smem] + [vmem] * 10,
+        in_specs=[smem, smem, pl.BlockSpec(memory_space=pl.ANY)] + [vmem] * 9,
         out_specs=[vmem, vmem],
         scratch_shapes=[
             pltpu.VMEM((NT, 128, G), F32),
@@ -480,7 +479,10 @@
             pltpu.VMEM((NT, 2, ROWS, 2 * ROWS), BF16),
             pltpu.VMEM((1024, 256), F32),
             pltpu.VMEM((NT, 128), F32),
+            pltpu.VMEM((8, NT, 128), F32),
             pltpu.VMEM((2, 8, G // 2), F32),
+            pltpu.VMEM((NT, 40, 128), BF16),
+            pltpu.SemaphoreType.DMA,
         ],
         compiler_params=pltpu.CompilerParams(vmem_limit_bytes=55 << 20),
     )(
@@ -499,8 +501,9 @@
     )
 
 
-def exchanged(value, axis, mask):
-    return lax.ppermute(value, axis, [(i, i ^ mask) for i in range(lax.axis_size(axis))])
+def exchanged(value, axis, masks):
+    size = lax.axis_size(axis)
+    return lax.ppermute(value, axis, [(i, i ^ masks[i % 2]) for i in range(size)])
 
 
 def on_device(tilt_images, anchors, euler, tilt_angle, defocus, warp, centers, amplitudes, widths):
@@ -508,14 +511,14 @@
     received = lax.all_to_all(payload, "tilt", split_axis=0, concat_axis=0, tiled=True)
     index = lax.axis_index("tilt").astype(jnp.int32)
     total, other = work(index.reshape(1), euler, received, centers, amplitudes, widths)
-    total = total + exchanged(other, "tilt", 1)
-    for mask in (2, 6, 8, 24):
-        total = total + exchanged(total, "tilt", mask)
+    total = total + exchanged(other, "tilt", (1, 1))
+    for masks in ((2, 8), (6, 24), (8, 2), (24, 6)):
+        total = total + exchanged(total, "tilt", masks)
     place = index // 2
     warp_local = lax.dynamic_slice(total, (5 + place // 8, (place % 8) * 128), (1, 6))
-    for mask in (1, 2, 7):
-        total = total + exchanged(total, "tomo", mask)
-    other = exchanged(total, "tilt", 1)
+    for mask in (1, 2, 6):
+        total = total + exchanged(total, "tomo", (mask, mask))
+    other = exchanged(total, "tilt", (1, 1))
     first = index % 2 == 0
     template = jnp.concatenate(
         [jnp.where(first, total, other)[:5], jnp.where(first, other, total)[:5]], 1

time: 98.5 us -> 95.7 us (0.972)
  Pallas kernels: 38.8 us -> 35.4 us
    pallas_call x1, Pallas kernels: 7.71 us -> 4.22 us  [cut(): pl.pallas_call(cut_kernel, out_shape=jax.ShapeDtypeStruct((NP, 40, 128),...]
where the time goes in v3:
time: 95.7 us; the launch traced here: 95.3 us
  Pallas kernels  35.4 us (37%)
  starting transfers between devices  29.8 us (31%)
  waiting for transfers between devices  25.4 us (27%)
  between operations  1.97 us (2%)
  other arithmetic  1.45 us (2%)
  local copies, waits for them, and re-layouts  1.3 us (1%)
    pallas_call x1, Pallas kernels, work(): pl.pallas_call(work_kernel, out_shape=[jax.ShapeDtypeStruct((8, G // 2),...  31.2 us
    ppermute x9, starting transfers between devices, exchanged(): lax.ppermute(value, axis, [(i, i ^ masks[i % 2]) for i in range(size)])  21.2 us
    ppermute x9, waiting for transfers between devices, exchanged(): lax.ppermute(value, axis, [(i, i ^ masks[i % 2]) for i in range(size)])  15.9 us
    all_to_all x1, waiting for transfers between devices, on_device(): lax.all_to_all(payload, 'tilt', split_axis=0, concat_axis=0, tiled=True)  9.53 us
    all_to_all x1, starting transfers between devices, on_device(): lax.all_to_all(payload, 'tilt', split_axis=0, concat_axis=0, tiled=True)  8.6 us
    pallas_call x1, Pallas kernels, cut(): pl.pallas_call(cut_kernel, out_shape=jax.ShapeDtypeStruct((NP, 40, 128),...  4.22 us
  transfers between devices with their start and end apart: 10, of which 10 were waited for; matrix products, arithmetic and copies ran while one was open for 1% of the time, Pallas kernels for 0%

profile of v3, /device:TPU:1, one launch (start us, length us, event | category | flops | bytes accessed | tf_op | source)
XLA Modules:
  0.0 95.3 jit_solution(11035849469923667767)
XLA Ops:
  1.9 4.2 %shard_map.158 = bf16[32,40,128]{2,1,0:T(8,128)(2,1)} custom-call(s32[1,1,2,32]{3,2,1,0:T(2,128)} %bitcast.10, f32[1,1]{1,0:T(1,128)S(6)} %copy.17.angle, f32[1,1]{1,0:T(1,128)S(6)} %copy.18.focus, f32[1,1,6]{2,1,0:T(1,128)} %warp.1, bf16[1,1,1024,1024]{3,2,1,0:T(8,128)(2,1)} %image.1), custom_call_target="tpu_custom_call" | custom-call | tf_op jit(solution)/shard_map/pallas_call | solution.py:134
  6.2 8.6 %all-to-all-start = ((bf16[32,40,128]{2,1,0:T(8,128)(2,1)}), bf16[32,40,128]{2,1,0:T(8,128)(2,1)S(1)}, u32[]{:S(2)}, u32[]{:S(2)}) async-start(bf16[32,40,128]{2,1,0:T(8,128)(2,1)} %shard_map.158), calls=%async_computation | async-start | bytes 655360 | tf_op jit(solution)/shard_map/all_to_all | solution.py:511
  14.8 9.5 %all-to-all-done.incoming = bf16[32,40,128]{2,1,0:T(8,128)(2,1)S(1)} async-done(((bf16[32,40,128]{2,1,0:T(8,128)(2,1)}), bf16[32,40,128]{2,1,0:T(8,128)(2,1)S(1)}, u32[]{:S(2)}, u32[]{:S(2)}) %all-to-all-start) | async-done | bytes 327712 | tf_op jit(solution)/shard_map/all_to_all | solution.py:511
  24.3 0.0 copy-start
  24.3 0.7 copy-done
  25.0 31.2 %shard_map.159 = (f32[8,1024]{1,0:T(8,128)}, f32[8,1024]{1,0:T(8,128)}) custom-call(s32[1]{0:T(128)} %bitcast.slot, f32[3,1,32]{2,1,0:T(1,128)} %bitcast.9, bf16[32,40,128]{2,1,0:T(8,128)(2,1)} %copy-done, f32[3,2048]{1,0:T(4,128)} %centers.1, f32[1,2048]{1,0:T(1,128)} %bitcast.7, f32[1,2048]{1,0:T(1,128)} %bitcast.8, ...), custom_call_target="tpu_custom_call" | custom-call | tf_op jit(solution)/shard_map/pallas_call | solution.py:464
  56.2 0.4 collective-permute-start
  56.6 1.1 %collective-permute-done = f32[8,1024]{1,0:T(8,128)S(1)} collective-permute-done((f32[8,1024]{1,0:T(8,128)}, f32[8,1024]{1,0:T(8,128)S(1)}, u32[]{:S(2)}, u32[]{:S(2)}) %collective-permute-start) | collective-permute-done | bytes 32800 | tf_op jit(solution)/shard_map/ppermute | solution.py:506
  57.7 0.8 add.42
  58.5 0.3 collective-permute-start.1
  58.8 2.4 %collective-permute-done.1 = f32[8,1024]{1,0:T(8,128)S(1)} collective-permute-done((f32[8,1024]{1,0:T(8,128)S(1)}, f32[8,1024]{1,0:T(8,128)S(1)}, u32[]{:S(2)}, u32[]{:S(2)}) %collective-permute-start.1) | collective-permute-done | bytes 32800 | tf_op jit(solution)/shard_map/ppermute | solution.py:506
  61.3 0.9 collective-permute-start.2
  62.1 3.1 %collective-permute-done.2 = f32[8,1024]{1,0:T(8,128)S(1)} collective-permute-done((f32[8,1024]{1,0:T(8,128)S(1)}, f32[8,1024]{1,0:T(8,128)S(1)}, u32[]{:S(2)}, u32[]{:S(2)}) %collective-permute-start.2) | collective-permute-done | bytes 32800 | tf_op jit(solution)/shard_map/ppermute | solution.py:506
  65.2 0.5 collective-permute-start.3
  65.8 2.3 %collective-permute-done.3 = f32[8,1024]{1,0:T(8,128)S(1)} collective-permute-done((f32[8,1024]{1,0:T(8,128)S(1)}, f32[8,1024]{1,0:T(8,128)S(1)}, u32[]{:S(2)}, u32[]{:S(2)}) %collective-permute-start.3) | collective-permute-done | bytes 32800 | tf_op jit(solution)/shard_map/ppermute | solution.py:506
  68.0 1.2 %collective-permute-start.4 = (f32[8,1024]{1,0:T(8,128)S(1)}, f32[8,1024]{1,0:T(8,128)S(1)}, u32[]{:S(2)}, u32[]{:S(2)}) collective-permute-start(f32[8,1024]{1,0:T(8,128)S(1)} %add.45), channel_id=1, source_target_pairs={{0,24},{1,7},{2,26},{3,5},{4,28},{5,3},{6,30},{7,1},{8,16},{9,15},... | collective-permute-start | bytes 98312 | tf_op jit(solution)/shard_map/ppermute | solution.py:506
  69.2 2.8 %collective-permute-done.4 = f32[8,1024]{1,0:T(8,128)S(1)} collective-permute-done((f32[8,1024]{1,0:T(8,128)S(1)}, f32[8,1024]{1,0:T(8,128)S(1)}, u32[]{:S(2)}, u32[]{:S(2)}) %collective-permute-start.4) | collective-permute-done | bytes 32800 | tf_op jit(solution)/shard_map/ppermute | solution.py:506
  72.0 1.6 %collective-permute-start.5 = (f32[8,1024]{1,0:T(8,128)S(1)}, f32[8,1024]{1,0:T(8,128)S(1)}, u32[]{:S(2)}, u32[]{:S(2)}) collective-permute-start(f32[8,1024]{1,0:T(8,128)S(1)} %add.46), channel_id=1, source_target_pairs={{0,32},{32,0},{64,96},{96,64},{128,160},{160,128},{192,224},{224,1... | collective-permute-start | bytes 98312 | tf_op jit(solution)/shard_map/ppermute | solution.py:506
  73.6 1.3 %collective-permute-done.5 = f32[8,1024]{1,0:T(8,128)S(1)} collective-permute-done((f32[8,1024]{1,0:T(8,128)S(1)}, f32[8,1024]{1,0:T(8,128)S(1)}, u32[]{:S(2)}, u32[]{:S(2)}) %collective-permute-start.5) | collective-permute-done | bytes 32800 | tf_op jit(solution)/shard_map/ppermute | solution.py:506
  74.9 3.0 %collective-permute-start.6 = (f32[8,1024]{1,0:T(8,128)S(1)}, f32[8,1024]{1,0:T(8,128)S(1)}, u32[]{:S(2)}, u32[]{:S(2)}) collective-permute-start(f32[8,1024]{1,0:T(8,128)S(1)} %add.47), channel_id=1, source_target_pairs={{0,64},{32,96},{64,0},{96,32},{128,192},{160,224},{192,128},{224,1... | collective-permute-start | bytes 98312 | tf_op jit(solution)/shard_map/ppermute | solution.py:506
  77.9 1.3 %collective-permute-done.6 = f32[8,1024]{1,0:T(8,128)S(1)} collective-permute-done((f32[8,1024]{1,0:T(8,128)S(1)}, f32[8,1024]{1,0:T(8,128)S(1)}, u32[]{:S(2)}, u32[]{:S(2)}) %collective-permute-start.6) | collective-permute-done | bytes 32800 | tf_op jit(solution)/shard_map/ppermute | solution.py:506
  79.2 5.2 %collective-permute-start.7 = (f32[8,1024]{1,0:T(8,128)S(1)}, f32[8,1024]{1,0:T(8,128)S(1)}, u32[]{:S(2)}, u32[]{:S(2)}) collective-permute-start(f32[8,1024]{1,0:T(8,128)S(1)} %add.48), channel_id=1, source_target_pairs={{0,192},{32,224},{64,128},{96,160},{128,64},{160,96},{192,0},{224,... | collective-permute-start | bytes 98312 | tf_op jit(solution)/shard_map/ppermute | solution.py:506
  84.5 1.3 %collective-permute-done.7 = f32[8,1024]{1,0:T(8,128)S(1)} collective-permute-done((f32[8,1024]{1,0:T(8,128)S(1)}, f32[8,1024]{1,0:T(8,128)S(1)}, u32[]{:S(2)}, u32[]{:S(2)}) %collective-permute-start.7) | collective-permute-done | bytes 32800 | tf_op jit(solution)/shard_map/ppermute | solution.py:506
  85.8 8.1 %collective-permute-start.8 = (f32[8,1024]{1,0:T(8,128)S(1)}, f32[8,1024]{1,0:T(8,128)S(1)}, u32[]{:S(2)}, u32[]{:S(2)}) collective-permute-start(f32[8,1024]{1,0:T(8,128)S(1)} %add.49), channel_id=1, source_target_pairs={{0,1},{1,0},{2,3},{3,2},{4,5},{5,4},{6,7},{7,6},{8,9},{9,8},{10,11... | collective-permute-start | bytes 98312 | tf_op jit(solution)/shard_map/ppermute | solution.py:506
  93.8 0.6 dynamic-slice_bitcast_fusion
  94.4 0.3 collective-permute-done.8
  94.7 0.6 pad_maximum_fusion
  (8 shorter events, 0.0 us)
Async XLA Ops:
  6.2 18.1 %all-to-all-start = ((bf16[32,40,128]{2,1,0:T(8,128)(2,1)}), bf16[32,40,128]{2,1,0:T(8,128)(2,1)S(1)}, u32[]{:S(2)}, u32[]{:S(2)}) async-start(bf16[32,40,128]{2,1,0:T(8,128)(2,1)} %shard_map.158), calls=%async_computation | async-start | bytes 655360 | tf_op jit(solution)/shard_map/all_to_all | solution.py:511
  24.3 0.7 copy-start
  56.2 1.5 %collective-permute-start = (f32[8,1024]{1,0:T(8,128)}, f32[8,1024]{1,0:T(8,128)S(1)}, u32[]{:S(2)}, u32[]{:S(2)}) collective-permute-start(f32[8,1024]{1,0:T(8,128)} %get-tuple-element.5), channel_id=1, source_target_pairs={{0,1},{1,0},{2,3},{3,2},{4,5},{5,4},{6,7},{7,6},{8,9},{9,8},{10,11... | collective-permute-start | bytes 98312 | tf_op jit(solution)/shard_map/ppermute | solution.py:506
  58.5 2.8 %collective-permute-start.1 = (f32[8,1024]{1,0:T(8,128)S(1)}, f32[8,1024]{1,0:T(8,128)S(1)}, u32[]{:S(2)}, u32[]{:S(2)}) collective-permute-start(f32[8,1024]{1,0:T(8,128)S(1)} %add.42), channel_id=1, source_target_pairs={{0,2},{1,9},{2,0},{3,11},{4,6},{5,13},{6,4},{7,15},{8,10},{9,1},{1... | collective-permute-start | bytes 98312 | tf_op jit(solution)/shard_map/ppermute | solution.py:506
  61.3 4.0 %collective-permute-start.2 = (f32[8,1024]{1,0:T(8,128)S(1)}, f32[8,1024]{1,0:T(8,128)S(1)}, u32[]{:S(2)}, u32[]{:S(2)}) collective-permute-start(f32[8,1024]{1,0:T(8,128)S(1)} %add.43), channel_id=1, source_target_pairs={{0,6},{1,25},{2,4},{3,27},{4,2},{5,29},{6,0},{7,31},{8,14},{9,17},... | collective-permute-start | bytes 98312 | tf_op jit(solution)/shard_map/ppermute | solution.py:506
  65.2 2.8 %collective-permute-start.3 = (f32[8,1024]{1,0:T(8,128)S(1)}, f32[8,1024]{1,0:T(8,128)S(1)}, u32[]{:S(2)}, u32[]{:S(2)}) collective-permute-start(f32[8,1024]{1,0:T(8,128)S(1)} %add.44), channel_id=1, source_target_pairs={{0,8},{1,3},{2,10},{3,1},{4,12},{5,7},{6,14},{7,5},{8,0},{9,11},{1... | collective-permute-start | bytes 98312 | tf_op jit(solution)/shard_map/ppermute | solution.py:506
  68.0 4.0 %collective-permute-start.4 = (f32[8,1024]{1,0:T(8,128)S(1)}, f32[8,1024]{1,0:T(8,128)S(1)}, u32[]{:S(2)}, u32[]{:S(2)}) collective-permute-start(f32[8,1024]{1,0:T(8,128)S(1)} %add.45), channel_id=1, source_target_pairs={{0,24},{1,7},{2,26},{3,5},{4,28},{5,3},{6,30},{7,1},{8,16},{9,15},... | collective-permute-start | bytes 98312 | tf_op jit(solution)/shard_map/ppermute | solution.py:506
  72.0 2.9 %collective-permute-start.5 = (f32[8,1024]{1,0:T(8,128)S(1)}, f32[8,1024]{1,0:T(8,128)S(1)}, u32[]{:S(2)}, u32[]{:S(2)}) collective-permute-start(f32[8,1024]{1,0:T(8,128)S(1)} %add.46), channel_id=1, source_target_pairs={{0,32},{32,0},{64,96},{96,64},{128,160},{160,128},{192,224},{224,1... | collective-permute-start | bytes 98312 | tf_op jit(solution)/shard_map/ppermute | solution.py:506
  74.9 4.3 %collective-permute-start.6 = (f32[8,1024]{1,0:T(8,128)S(1)}, f32[8,1024]{1,0:T(8,128)S(1)}, u32[]{:S(2)}, u32[]{:S(2)}) collective-permute-start(f32[8,1024]{1,0:T(8,128)S(1)} %add.47), channel_id=1, source_target_pairs={{0,64},{32,96},{64,0},{96,32},{128,192},{160,224},{192,128},{224,1... | collective-permute-start | bytes 98312 | tf_op jit(solution)/shard_map/ppermute | solution.py:506
  79.2 6.5 %collective-permute-start.7 = (f32[8,1024]{1,0:T(8,128)S(1)}, f32[8,1024]{1,0:T(8,128)S(1)}, u32[]{:S(2)}, u32[]{:S(2)}) collective-permute-start(f32[8,1024]{1,0:T(8,128)S(1)} %add.48), channel_id=1, source_target_pairs={{0,192},{32,224},{64,128},{96,160},{128,64},{160,96},{192,0},{224,... | collective-permute-start | bytes 98312 | tf_op jit(solution)/shard_map/ppermute | solution.py:506
  85.8 8.9 %collective-permute-start.8 = (f32[8,1024]{1,0:T(8,128)S(1)}, f32[8,1024]{1,0:T(8,128)S(1)}, u32[]{:S(2)}, u32[]{:S(2)}) collective-permute-start(f32[8,1024]{1,0:T(8,128)S(1)} %add.49), channel_id=1, source_target_pairs={{0,1},{1,0},{2,3},{3,2},{4,5},{5,4},{6,7},{7,6},{8,9},{9,8},{10,11... | collective-permute-start | bytes 98312 | tf_op jit(solution)/shard_map/ppermute | solution.py:506

commit v4 on v3

--- a/solution.py
+++ b/solution.py
@@ -13,11 +13,13 @@
 IMG = 1024
 NT = 32
 NP = 32
+SHARES = 16
+CHUNK = G // SHARES
 CH = 256
 NCH = G // CH
 HALF = 40
 ROWS = 2 * HALF
-UF, US, UR, UB = 2, 8, 8, 2
+UF, UB = 3, 4
 F32 = jnp.float32
 BF16 = jnp.bfloat16
 
@@ -97,8 +99,13 @@
 
 
 def cut_kernel(anchor, angle, focus, warp, image, out, held, sem, strip):
-    copy = pltpu.make_async_copy(image.at[0, 0], held, sem)
-    copy.start()
+    bands = [pl.ds(i * (IMG // 8), IMG // 8) for i in range(8)]
+    copies = [
+        pltpu.make_async_copy(image.at[0, 0, band], held.at[band], sem.at[i])
+        for i, band in enumerate(bands)
+    ]
+    for copy in copies:
+        copy.start()
     lane = lax.broadcasted_iota(jnp.int32, (8, 128), 1)
     sub = lax.broadcasted_iota(jnp.int32, (8, 128), 0)
     values = [angle[0, 0], focus[0, 0]] + [warp[0, 0, i] for i in range(6)]
@@ -111,7 +118,8 @@
     parts = jnp.where(sub == 0, hi, jnp.where(sub == 1, mid, jnp.where(sub == 2, low, 0.0)))
     left_half = lax.broadcasted_iota(jnp.int32, (32, 128), 1) < BOX
 
-    copy.wait()
+    for copy in copies:
+        copy.wait()
 
     def one(p, carry):
         r, c = anchor[0, 0, 0, p], anchor[0, 0, 1, p]
@@ -138,7 +146,7 @@
         out_specs=pl.BlockSpec(memory_space=pltpu.VMEM),
         scratch_shapes=[
             pltpu.VMEM((IMG, IMG), BF16),
-            pltpu.SemaphoreType.DMA,
+            pltpu.SemaphoreType.DMA((8,)),
             pltpu.VMEM((8, 80, 128), F32),
         ],
         compiler_params=pltpu.CompilerParams(vmem_limit_bytes=55 << 20),
@@ -158,8 +166,7 @@
     joiner,
     chooser,
     aux,
-    keep,
-    send,
+    out,
     xs,
     base,
     step,
@@ -170,17 +177,18 @@
     model,
     spectra,
     mats,
-    zsc,
     focus,
     cols,
-    out,
     received,
+    raw,
     sem,
 ):
     copy = pltpu.make_async_copy(incoming, received, sem)
     copy.start()
     copy.wait()
-    prm = jnp.sum(received[:, 32:40, :].astype(F32), axis=1)
+    raw[...] = received[:, 32:40, :].astype(F32).reshape(NT * 8, 128)
+    prm = raw[pl.ds(0, NT, stride=8), :] + raw[pl.ds(1, NT, stride=8), :]
+    prm = prm + raw[pl.ds(2, NT, stride=8), :]
     focus[...] = jnp.broadcast_to(prm[:, 1:2], (NT, 128))
     ct, st = cos_sin_turns(prm * (0.5 / math.pi))
     firsts = (ct[:, 0:1], st[:, 0:1])
@@ -208,7 +216,31 @@
     freq32 = lax.broadcasted_iota(jnp.int32, (32, CH), 0).astype(F32)
     first = lax.broadcasted_iota(jnp.int32, (8, CH), 0) == 0
 
-    def prepare(c, carry):
+    lane = lax.broadcasted_iota(jnp.int32, (HALF, 128), 1)
+    sign = jnp.where(lane < 64, 1.0, -1.0)
+
+    def swap(x):
+        return pltpu.roll(x, 64, 1)
+
+    def spectrum(c, sums):
+        rows = received[pl.ds(c * 4, 4), 0:32, :].reshape(128, 128)
+        halves = jnp.dot(rows, right_hi[...], preferred_element_type=F32)
+        halves = halves + jnp.dot(rows, right_lo[...], preferred_element_type=F32)
+        for i in range(4):
+            z = halves[32 * i : 32 * i + 32]
+            z = jnp.concatenate([z[:, :128], z[:, 128:]], 0)
+            z_hi, z_lo = split(z)
+            p = jnp.dot(
+                left[...], jnp.concatenate([z_hi, z_lo, z_hi], 0), preferred_element_type=F32
+            )
+            pc, ps = p[:HALF], swap(p[HALF:])
+            spectra[c * 4 + i, :HALF] = pc
+            spectra[c * 4 + i, HALF:] = ps
+            plus, minus = sign * pc - ps, pc + sign * ps
+            sums = sums[0] + plus * plus, sums[1] + minus * minus
+        return sums
+
+    def prepare(c, sums):
         sl = pl.ds(pl.multiple_of(c * CH, CH), CH)
         r0, r1, r2 = rotated(sl)
         ct, st, a00, a01, a10, a11, sh_x, sh_y = (
@@ -252,9 +284,13 @@
                     lanes = slice(i * 128, i * 128 + 128)
                     base[2 * axis, tile, pl.ds(j, NT, stride=8), :] = e[0][:, lanes]
                     base[2 * axis + 1, tile, pl.ds(j, NT, stride=8), :] = e[1][:, lanes]
-        return carry
-
-    lax.fori_loop(0, NCH, prepare, 0)
+        return spectrum(c, sums)
+
+    nought = jnp.zeros((HALF, 128), F32)
+    plus, minus = lax.fori_loop(0, NCH, prepare, (nought, nought), unroll=2)
+    f_plus = aux[1] / (0.25 + (plus + swap(plus)) * (1.0 / NT))
+    f_minus = aux[2] / (0.25 + (minus + swap(minus)) * (1.0 / NT))
+    radius = aux[0]
 
     blank = jnp.zeros((24, CH), F32)
 
@@ -283,7 +319,7 @@
         sn = jnp.where(first, nyq[2 * axis + 1, pl.ds(k, 1), sl], 0.0)
         return [cn], [sn]
 
-    def forward(b, carry):
+    def forward(b):
         total = jnp.zeros((2 * ROWS, 256), F32)
         for c in range(NCH):
             sl = slice(c * CH, (c + 1) * CH)
@@ -303,40 +339,8 @@
             )
         model[2 * b] = total[:ROWS, :128]
         model[2 * b + 1] = total[ROWS:, 128:]
-        return carry
-
-    lax.fori_loop(0, NT // 2, forward, 0, unroll=UF)
-
-    for b in range(4):
-        rows = received[8 * b : 8 * b + 8, 0:32, :].reshape(256, 128)
-        zsc[256 * b : 256 * b + 256, :] = jnp.dot(
-            rows, right_hi[...], preferred_element_type=F32
-        ) + jnp.dot(rows, right_lo[...], preferred_element_type=F32)
-
-    lane = lax.broadcasted_iota(jnp.int32, (HALF, 128), 1)
-    sign = jnp.where(lane < 64, 1.0, -1.0)
-
-    def swap(x):
-        return pltpu.roll(x, 64, 1)
-
-    def spectrum(k, sums):
-        z = zsc[pl.ds(pl.multiple_of(k * 32, 32), 32), :]
-        z = jnp.concatenate([z[:, :128], z[:, 128:]], 0)
-        z_hi, z_lo = split(z)
-        p = jnp.dot(left[...], jnp.concatenate([z_hi, z_lo, z_hi], 0), preferred_element_type=F32)
-        pc, ps = p[:HALF], swap(p[HALF:])
-        spectra[k, :HALF] = pc
-        spectra[k, HALF:] = ps
-        plus, minus = sign * pc - ps, pc + sign * ps
-        return sums[0] + plus * plus, sums[1] + minus * minus
-
-    nought = jnp.zeros((HALF, 128), F32)
-    plus, minus = lax.fori_loop(0, NT, spectrum, (nought, nought), unroll=US)
-    f_plus = aux[1] / (0.25 + (plus + swap(plus)) * (1.0 / NT))
-    f_minus = aux[2] / (0.25 + (minus + swap(minus)) * (1.0 / NT))
-    radius = aux[0]
-
-    def residual(k, carry):
+
+    def residual(k):
         x = focus[pl.ds(k, 1), :] * radius * (1.0 / BOX) + 0.1
         n = jnp.round(x * (0.5 / math.pi))
         r = (x - n * 6.28125) - n * (2.0 * math.pi - 6.28125)
@@ -356,9 +360,17 @@
             (((1,), (1,)), ((), ())),
             preferred_element_type=F32,
         ).astype(BF16)
+
+    def pair(b, carry):
+        forward(b + 1)
+        residual(2 * b)
+        residual(2 * b + 1)
         return carry
 
-    lax.fori_loop(0, NT, residual, 0, unroll=UR)
+    forward(0)
+    lax.fori_loop(0, NT // 2 - 1, pair, 0, unroll=UF)
+    residual(NT - 2)
+    residual(NT - 1)
 
     acc[...] = jnp.zeros_like(acc)
     w1 = [freq8 + float(8 * m) for m in range(4)]
@@ -375,36 +387,33 @@
                 cn, sn = ends_of(k, axis, sl)
                 parts.append((cs, ss))
                 sides.append(jnp.concatenate(cs + cn + ss + sn, 0).astype(BF16))
-            backs = [
-                jnp.dot(
+            width_sum = acc[0, :, sl]
+            for axis in (0, 1):
+                back = jnp.dot(
                     mats[k, axis],
                     jnp.concatenate([sides[1 - axis]] * 2, 0),
                     preferred_element_type=F32,
                 )
-                for axis in (0, 1)
-            ]
-            width_sum = acc[0, :, sl]
-            value_sum = acc[1, :, sl]
-            moves = [None, None]
-            for m in range(4):
-                values = []
-                for axis in (0, 1):
-                    c_m, s_m = parts[axis][0][m], parts[axis][1][m]
-                    kc = backs[axis][8 * m : 8 * m + 8]
-                    ks = backs[axis][HALF + 8 * m : HALF + 8 * m + 8]
-                    values.append(c_m * kc + s_m * ks)
-                    move = w1[m] * (c_m * ks - s_m * kc)
-                    moves[axis] = move if m == 0 else moves[axis] + move
-                value_sum = value_sum + values[1]
-                width_sum = width_sum + w2[m] * (values[0] + values[1])
+                cs, ss = parts[axis]
+                move = None
+                value_sum = acc[1, :, sl] if axis == 1 else None
+                for m in range(4):
+                    kc = back[8 * m : 8 * m + 8]
+                    ks = back[HALF + 8 * m : HALF + 8 * m + 8]
+                    re = cs[m] * kc + ss[m] * ks
+                    im = w1[m] * (cs[m] * ks - ss[m] * kc)
+                    width_sum = width_sum + w2[m] * re
+                    move = im if m == 0 else move + im
+                    if axis == 1:
+                        value_sum = value_sum + re
+                if axis == 1:
+                    acc[1, :, sl] = value_sum
+                for t in range(CH // 128):
+                    lanes = slice(t * 128, t * 128 + 128)
+                    base[axis, c * (CH // 128) + t, pl.ds(k8, 8), :] = move[:, lanes]
+                nyqk[2 * axis, pl.ds(k, 1), sl] = back[32:33]
+                nyqk[2 * axis + 1, pl.ds(k, 1), sl] = back[HALF + 32 : HALF + 33]
             acc[0, :, sl] = width_sum
-            acc[1, :, sl] = value_sum
-            for axis in (0, 1):
-                for i in range(CH // 128):
-                    lanes = slice(i * 128, i * 128 + 128)
-                    base[axis, c * (CH // 128) + i, pl.ds(k8, 8), :] = moves[axis][:, lanes]
-                nyqk[2 * axis, pl.ds(k, 1), sl] = backs[axis][32:33]
-                nyqk[2 * axis + 1, pl.ds(k, 1), sl] = backs[axis][HALF + 32 : HALF + 33]
         return carry
 
     lax.fori_loop(0, NT, backward, 0, unroll=UB)
@@ -438,23 +447,18 @@
         x, y = cc * x + sc * y, cc * y - sc * x
         curve = jnp.sum(acc[0, :, sl], axis=0, keepdims=True) + 1024.0 * (ends[0] + ends[1])
         value = jnp.sum(acc[1, :, sl], axis=0, keepdims=True) + ends[1]
-        half, lanes = c // 8, slice((c % 8) * 128, (c % 8) * 128 + 128)
-        out[half, 0:1, lanes] = x
-        out[half, 1:2, lanes] = y
-        out[half, 2:3, lanes] = z
-        out[half, 3:4, lanes] = value / amplitudes[0:1, sl]
-        out[half, 4:5, lanes] = (-2.0 * blur) * widths[0:1, sl] * curve
+        rows = (x, y, z, value / amplitudes[0:1, sl], (-2.0 * blur) * widths[0:1, sl] * curve)
+        for i, row in enumerate(rows):
+            out[c, 0:1, i * CHUNK : (i + 1) * CHUNK] = row
     lane_w = lax.broadcasted_iota(jnp.int32, (NT, 128), 1)
     warp_rows = jnp.zeros((NT, 128), F32)
     for i in range(6):
         total = jnp.sum(terms[i], axis=1, keepdims=True) * (20.0 if i > 3 else 1.0)
         warp_rows = jnp.where(lane_w == i, total, warp_rows)
-    for k in range(NT):
-        i = k // 2
-        out[k % 2, 5 + i // 8 : 6 + i // 8, (i % 8) * 128 : (i % 8) * 128 + 128] = warp_rows[k : k + 1]
-    core = mine % 2
-    keep[...] = out[core]
-    send[...] = out[1 - core]
+    moved_rows = pltpu.roll(warp_rows, 64, 1)
+    for d in range(SHARES):
+        k = 2 * d
+        out[d, 0:1, 5 * CHUNK : 6 * CHUNK] = warp_rows[k : k + 1] + moved_rows[k + 1 : k + 2]
 
 
 def work(slot, euler, received, centers, amplitudes, widths):
@@ -463,9 +467,9 @@
     right_hi, right_lo, left, joiner, chooser, aux = tables()
     return pl.pallas_call(
         work_kernel,
-        out_shape=[jax.ShapeDtypeStruct((8, G // 2), F32)] * 2,
+        out_shape=jax.ShapeDtypeStruct((SHARES, 1, 6 * CHUNK), F32),
         in_specs=[smem, smem, pl.BlockSpec(memory_space=pl.ANY)] + [vmem] * 9,
-        out_specs=[vmem, vmem],
+        out_specs=vmem,
         scratch_shapes=[
             pltpu.VMEM((NT, 128, G), F32),
             pltpu.VMEM((4, G // 128, NT * 8, 128), F32),
@@ -477,11 +481,10 @@
             pltpu.VMEM((NT, ROWS, 128), F32),
             pltpu.VMEM((NT, ROWS, 128), F32),
             pltpu.VMEM((NT, 2, ROWS, 2 * ROWS), BF16),
-            pltpu.VMEM((1024, 256), F32),
             pltpu.VMEM((NT, 128), F32),
             pltpu.VMEM((8, NT, 128), F32),
-            pltpu.VMEM((2, 8, G // 2), F32),
             pltpu.VMEM((NT, 40, 128), BF16),
+            pltpu.VMEM((NT * 8, 128), F32),
             pltpu.SemaphoreType.DMA,
         ],
         compiler_params=pltpu.CompilerParams(vmem_limit_bytes=55 << 20),
@@ -501,28 +504,35 @@
     )
 
 
-def exchanged(value, axis, masks):
-    size = lax.axis_size(axis)
-    return lax.ppermute(value, axis, [(i, i ^ masks[i % 2]) for i in range(size)])
-
-
 def on_device(tilt_images, anchors, euler, tilt_angle, defocus, warp, centers, amplitudes, widths):
+    tomos, cores = lax.axis_size("tomo"), lax.axis_size("tilt") // SHARES
+    row = [[(t * SHARES + i) * cores + c for i in range(SHARES)] for t in range(tomos) for c in range(cores)]
+    column = [[group[i] for group in row] for i in range(SHARES)]
+
+    def swapped(value, groups):
+        return lax.all_to_all(
+            value, ("tomo", "tilt"), split_axis=0, concat_axis=0, tiled=True, axis_index_groups=groups
+        )
+
+    index = lax.axis_index("tilt").astype(jnp.int32)
+    first = lax.axis_index("tomo").astype(jnp.int32) * cores
+    at = 5 * CHUNK + (index & 1) * 64
     payload = cut(tilt_images, anchors, tilt_angle, defocus, warp)
+    rest = (index, first, at, euler, centers, amplitudes, widths)
+    payload, rest = lax.optimization_barrier((payload, rest))
     received = lax.all_to_all(payload, "tilt", split_axis=0, concat_axis=0, tiled=True)
-    index = lax.axis_index("tilt").astype(jnp.int32)
-    total, other = work(index.reshape(1), euler, received, centers, amplitudes, widths)
-    total = total + exchanged(other, "tilt", (1, 1))
-    for masks in ((2, 8), (6, 24), (8, 2), (24, 6)):
-        total = total + exchanged(total, "tilt", masks)
-    place = index // 2
-    warp_local = lax.dynamic_slice(total, (5 + place // 8, (place % 8) * 128), (1, 6))
-    for mask in (1, 2, 6):
-        total = total + exchanged(total, "tomo", (mask, mask))
-    other = exchanged(total, "tilt", (1, 1))
-    first = index % 2 == 0
-    template = jnp.concatenate(
-        [jnp.where(first, total, other)[:5], jnp.where(first, other, total)[:5]], 1
-    )
+    received, rest = lax.optimization_barrier((received, rest))
+    index, first, at, euler, centers, amplitudes, widths = rest
+    partial = work(index.reshape(1), euler, received, centers, amplitudes, widths)
+    partial, first, at = lax.optimization_barrier((partial, first, at))
+    share = jnp.sum(swapped(partial, row), 0, keepdims=True)
+    shares = swapped(jnp.broadcast_to(share, (tomos * cores, 1, 6 * CHUNK)), column)
+    total = jnp.sum(shares, 0, keepdims=True)
+    chunks = swapped(jnp.broadcast_to(total, (SHARES, 1, 6 * CHUNK)), row)
+    chunks, shares, first, at = lax.optimization_barrier((chunks, shares, first, at))
+    template = chunks[:, 0, : 5 * CHUNK].reshape(SHARES, 5, CHUNK)
+    template = jnp.transpose(template, (1, 0, 2)).reshape(5, G)
+    warp_local = jnp.sum(lax.dynamic_slice(shares, (first, 0, at), (cores, 1, 6)), 0)
     return (template, warp_local.reshape(1, 1, 6))
 
 

time: 95.7 us -> 93 us (0.972)
  blocking collectives: 0 us -> 54.7 us
  starting transfers between devices: 29.8 us -> 0 us
  waiting for transfers between devices: 25.4 us -> 0 us
  Pallas kernels: 35.4 us -> 34.4 us
    all_to_all x0 -> x4, blocking collectives: none -> 54.7 us  [the longest x3 36.4 us: swapped(): lax.all_to_all(value, ('tomo', 'tilt'), split_axis=0, concat_axis=0, tile...]
    ppermute x9 -> x0, starting transfers between devices: 21.2 us -> none  [exchanged(): lax.ppermute(value, axis, [(i, i ^ masks[i % 2]) for i in range(size)])]
    ppermute x9 -> x0, waiting for transfers between devices: 15.9 us -> none  [exchanged(): lax.ppermute(value, axis, [(i, i ^ masks[i % 2]) for i in range(size)])]
    all_to_all x1 -> x0, waiting for transfers between devices: 9.53 us -> none  [on_device(): lax.all_to_all(payload, 'tilt', split_axis=0, concat_axis=0, tiled=True)]
    all_to_all x1 -> x0, starting transfers between devices: 8.6 us -> none  [on_device(): lax.all_to_all(payload, 'tilt', split_axis=0, concat_axis=0, tiled=True)]
  transfers between devices with their start and end apart: 10 -> 0, of which waited for: 10 -> 0; matrix products, arithmetic and copies ran while one was open for 1% -> 0% of each run, Pallas kernels for 0% -> 0%
where the time goes in v4:
time: 93 us; the launch traced here: 92.6 us
  blocking collectives  54.7 us (59%)
  Pallas kernels  34.4 us (37%)
  between operations  1.97 us (2%)
    all_to_all x3, blocking collectives, swapped(): lax.all_to_all(value, ('tomo', 'tilt'), split_axis=0, concat_axis=0, tile...  36.4 us
    pallas_call x1, Pallas kernels, work(): pl.pallas_call(work_kernel, out_shape=jax.ShapeDtypeStruct((SHARES, 1, 6...  30.2 us
    all_to_all x1, blocking collectives, on_device(): lax.all_to_all(payload, 'tilt', split_axis=0, concat_axis=0, tiled=True)  18.2 us
    pallas_call x1, Pallas kernels, cut(): pl.pallas_call(cut_kernel, out_shape=jax.ShapeDtypeStruct((NP, 40, 128),...  4.19 us

profile of v4, /device:TPU:1, one launch (start us, length us, event | category | flops | bytes accessed | tf_op | source)
XLA Modules:
  0.0 92.6 jit_solution(2885908946796264998)
XLA Ops:
  1.9 4.2 %shard_map.158 = bf16[32,40,128]{2,1,0:T(8,128)(2,1)} custom-call(s32[1,1,2,32]{3,2,1,0:T(2,128)} %bitcast.15, f32[1,1]{1,0:T(1,128)S(6)} %copy.20.angle, f32[1,1]{1,0:T(1,128)S(6)} %copy.21.focus, f32[1,1,6]{2,1,0:T(1,128)} %warp.1, bf16[1,1,1024,1024]{3,2,1,0:T(8,128)(2,1)} %image.1), custom_call_target="tpu_custom_call" | custom-call | tf_op jit(solution)/shard_map/pallas_call | solution.py:142
  6.1 18.2 %all_to_all.20.incoming = bf16[32,40,128]{2,1,0:T(8,128)(2,1)} all-to-all(bf16[32,40,128]{2,1,0:T(8,128)(2,1)} %shard_map.158), channel_id=1, replica_groups=mesh['tomo'=8,'tilt'=32] {'tilt'}, dimensions={0} | all-to-all | bytes 655360 | tf_op jit(solution)/shard_map/all_to_all | solution.py:523
  24.4 30.2 %shard_map.159 = f32[16,1,768]{2,1,0:T(1,128)} custom-call(s32[1]{0:T(128)} %bitcast.1.slot, f32[3,1,32]{2,1,0:T(1,128)} %bitcast.14, bf16[32,40,128]{2,1,0:T(8,128)(2,1)} %all_to_all.20.incoming, f32[3,2048]{1,0:T(4,128)} %centers, f32[1,2048]{1,0:T(1,128)} %bitcast.11, f32[1,2048]{1,0:T(1,128)} %bitcast.12, bf16[128,256]{1,0:T(8,128)(2,1)} %constant.37.clone.right_hi, ...), custom_call_target="tpu_custom_call" | custom-call | tf_op jit(solution)/shard_map/pallas_call | solution.py:468
  54.6 9.9 %all_to_all.21 = f32[16,1,768]{2,1,0:T(1,128)S(1)} all-to-all(f32[16,1,768]{2,1,0:T(1,128)} %shard_map.159), channel_id=1, replica_groups={{0,2,4,6,8,10,12,14,16,18,20,22,24,26,28,30},{1,3,5,7,9,11,13,15,17,19,..., dimensions={0} | all-to-all | bytes 98304 | tf_op jit(solution)/shard_map/all_to_all | solution.py:513
  64.6 17.2 %all_to_all.22 = f32[16,1,768]{2,1,0:T(1,128)S(1)} all-to-all(f32[16,1,768]{2,1,0:T(1,128)S(1)} %broadcast_in_dim.4), channel_id=1, replica_groups={{0,1,32,33,64,65,96,97,128,129,160,161,192,193,224,225},{2,3,34,35,66,6..., dimensions={0} | all-to-all | bytes 98304 | tf_op jit(solution)/shard_map/all_to_all | solution.py:513
  81.9 9.3 %all_to_all.23 = f32[16,1,768]{2,1,0:T(1,128)S(1)} all-to-all(f32[16,1,768]{2,1,0:T(1,128)S(1)} %broadcast_in_dim.5), channel_id=1, replica_groups={{0,2,4,6,8,10,12,14,16,18,20,22,24,26,28,30},{1,3,5,7,9,11,13,15,17,19,..., dimensions={0} | all-to-all | bytes 98304 | tf_op jit(solution)/shard_map/all_to_all | solution.py:513
  91.2 0.1 slice_reduce_fusion
  91.3 0.1 constant_dynamic-slice_fusion
  91.4 0.5 reduce_sum.29
  91.9 0.6 reshape_squeeze.3
  (4 shorter events, 0.1 us)

commit v5 on v4

--- a/solution.py
+++ b/solution.py
@@ -19,7 +19,7 @@
 NCH = G // CH
 HALF = 40
 ROWS = 2 * HALF
-UF, UB = 3, 4
+UF, UB = 3, 8
 F32 = jnp.float32
 BF16 = jnp.bfloat16
 
@@ -62,7 +62,7 @@
 
 def tables():
     pos = np.arange(BOX)
-    freq = np.arange(33)
+    freq = np.append(np.arange(1, 33), 0)
     ang = 2 * np.pi * ((pos[:, None] * freq[None, :]) % BOX) / BOX
     lanes = np.zeros((BOX, 128))
     lanes[:, :33] = np.cos(ang)
@@ -76,12 +76,11 @@
     rows[HALF : HALF + 33] = np.sin(ang).T / BOX
     left_hi, left_lo = np_split(rows)
     left = np.concatenate([left_hi, left_hi, left_lo], 1)
-    phi = np.ones(33)
-    phi[0] = phi[32] = 0.5
+    phi = np.where(freq % 32 == 0, 0.5, 1.0)
     both = -4.0 / (NT * NP) * phi[:, None] * phi[None, :]
     plus, minus = both.copy(), both.copy()
-    plus[32, 32] *= 2.0
-    minus[32, 32] = 0.0
+    plus[31, 31] *= 2.0
+    minus[31, 31] = 0.0
     aux = np.zeros((3, HALF, 128), np.float32)
     for base in (0, 64):
         aux[0, :33, base : base + 33] = freq[:, None] ** 2 + freq[None, :] ** 2
@@ -170,8 +169,7 @@
     xs,
     base,
     step,
-    nyq,
-    nyqk,
+    zero,
     env,
     acc,
     model,
@@ -212,8 +210,8 @@
         return x, y, z
 
     blur = 2.0 * math.pi**2 / BOX**2
-    freq8 = lax.broadcasted_iota(jnp.int32, (8, CH), 0).astype(F32)
-    freq32 = lax.broadcasted_iota(jnp.int32, (32, CH), 0).astype(F32)
+    freq8 = lax.broadcasted_iota(jnp.int32, (8, CH), 0).astype(F32) + 1.0
+    freq32 = lax.broadcasted_iota(jnp.int32, (32, CH), 0).astype(F32) + 1.0
     first = lax.broadcasted_iota(jnp.int32, (8, CH), 0) == 0
 
     lane = lax.broadcasted_iota(jnp.int32, (HALF, 128), 1)
@@ -253,7 +251,8 @@
         damp = jnp.exp(wide * (freq32 * freq32))
         env[0, :, sl] = damp
         env[1, :, sl] = amplitudes[0:1, sl] * damp
-        damp32 = jnp.exp(wide * 1024.0)
+        zero[0, :, sl] = jnp.where(first, 1.0, 0.0)
+        zero[1, :, sl] = jnp.where(first, amplitudes[0:1, sl], 0.0)
         for axis, u in ((0, ux), (1, uy)):
             u = u - jnp.round(u)
             c1, s1 = cos_sin_turns(u)
@@ -271,14 +270,9 @@
             e6 = twice(e3)
             e7 = times(e4, e3)
             c8, s8 = e8 = twice(e4)
-            cn, sn = twice(twice(e8))
-            d32 = damp32 if axis == 0 else amplitudes[0:1, sl] * damp32
-            nyq[2 * axis, :, sl] = cn * d32
-            nyq[2 * axis + 1, :, sl] = sn * d32
             step[2 * axis, :, sl] = c8
             step[2 * axis + 1, :, sl] = s8
-            e0 = (jnp.ones_like(c1), jnp.zeros_like(c1))
-            for j, e in enumerate((e0, e1, e2, e3, e4, e5, e6, e7)):
+            for j, e in enumerate((e1, e2, e3, e4, e5, e6, e7, e8)):
                 for i in range(CH // 128):
                     tile = c * (CH // 128) + i
                     lanes = slice(i * 128, i * 128 + 128)
@@ -314,31 +308,29 @@
                 gc, gs = gc * rc - gs * rs, gc * rs + gs * rc
         return cs, ss
 
-    def ends_of(k, axis, sl):
-        cn = jnp.where(first, nyq[2 * axis, pl.ds(k, 1), sl], 0.0)
-        sn = jnp.where(first, nyq[2 * axis + 1, pl.ds(k, 1), sl], 0.0)
-        return [cn], [sn]
-
     def forward(b):
-        total = jnp.zeros((2 * ROWS, 256), F32)
+        total = jnp.zeros((144, 256), F32)
         for c in range(NCH):
             sl = slice(c * CH, (c + 1) * CH)
             left_rows, right_rows = [], []
             for k in (2 * b, 2 * b + 1):
                 cs, ss = factors(k, 0, c)
-                cn, sn = ends_of(k, 0, sl)
-                left_rows += cs + cn + ss + sn
+                left_rows += cs + ss
                 cs, ss = factors(k, 1, c)
-                cn, sn = ends_of(k, 1, sl)
-                right_rows += cs + cn + [blank] + ss + sn + [blank]
+                right_rows += cs + [zero[1, :, sl], blank] + ss + [blank, blank[:8]]
+            left_rows += [zero[0, :, sl], blank[:8]]
             total = total + lax.dot_general(
                 jnp.concatenate(left_rows, 0).astype(BF16),
                 jnp.concatenate(right_rows, 0).astype(BF16),
                 (((1,), (1,)), ((), ())),
                 preferred_element_type=F32,
             )
-        model[2 * b] = total[:ROWS, :128]
-        model[2 * b + 1] = total[ROWS:, 128:]
+        for i in range(2):
+            lanes = slice(128 * i, 128 * i + 128)
+            model[2 * b + i, :32] = total[64 * i : 64 * i + 32, lanes]
+            model[2 * b + i, 32:HALF] = total[128:136, lanes]
+            model[2 * b + i, HALF : HALF + 32] = total[64 * i + 32 : 64 * i + 64, lanes]
+            model[2 * b + i, HALF + 32 :] = jnp.zeros((8, 128), F32)
 
     def residual(k):
         x = focus[pl.ds(k, 1), :] * radius * (1.0 / BOX) + 0.1
@@ -351,15 +343,16 @@
         hm = (f_minus * ctf) * (dc + sign * ds)
         m1 = jnp.concatenate([hm, swap(sign * hm)], 0).astype(BF16)
         m2 = jnp.concatenate([sign * hp, -swap(hp)], 0).astype(BF16)
-        mats[k, 0] = jnp.dot(
-            jnp.concatenate([m1, m2], 1), joiner[...], preferred_element_type=F32
-        ).astype(BF16)
-        mats[k, 1] = lax.dot_general(
+        back_x = jnp.dot(jnp.concatenate([m1, m2], 1), joiner[...], preferred_element_type=F32)
+        back_y = lax.dot_general(
             chooser[...],
             jnp.concatenate([m1, m2], 0),
             (((1,), (1,)), ((), ())),
             preferred_element_type=F32,
-        ).astype(BF16)
+        )
+        for axis, back in enumerate((back_x, back_y)):
+            rows = [back[:32], back[HALF : HALF + 32], back[32:HALF], back[HALF + 32 :]]
+            mats[k, axis] = jnp.concatenate(rows, 0).astype(BF16)
 
     def pair(b, carry):
         forward(b + 1)
@@ -384,13 +377,13 @@
             for axis in (0, 1):
                 cs = [xs[k, axis * 64 + 8 * m : axis * 64 + 8 * m + 8, sl] for m in range(4)]
                 ss = [xs[k, axis * 64 + 32 + 8 * m : axis * 64 + 40 + 8 * m, sl] for m in range(4)]
-                cn, sn = ends_of(k, axis, sl)
                 parts.append((cs, ss))
-                sides.append(jnp.concatenate(cs + cn + ss + sn, 0).astype(BF16))
+                rows = cs + [zero[axis, :, sl]] + ss + [blank[:8]]
+                sides.append(jnp.concatenate(rows, 0).astype(BF16))
             width_sum = acc[0, :, sl]
             for axis in (0, 1):
                 back = jnp.dot(
-                    mats[k, axis],
+                    mats[k, axis, : 64 + 16 * axis],
                     jnp.concatenate([sides[1 - axis]] * 2, 0),
                     preferred_element_type=F32,
                 )
@@ -399,7 +392,7 @@
                 value_sum = acc[1, :, sl] if axis == 1 else None
                 for m in range(4):
                     kc = back[8 * m : 8 * m + 8]
-                    ks = back[HALF + 8 * m : HALF + 8 * m + 8]
+                    ks = back[32 + 8 * m : 40 + 8 * m]
                     re = cs[m] * kc + ss[m] * ks
                     im = w1[m] * (cs[m] * ks - ss[m] * kc)
                     width_sum = width_sum + w2[m] * re
@@ -407,12 +400,10 @@
                     if axis == 1:
                         value_sum = value_sum + re
                 if axis == 1:
-                    acc[1, :, sl] = value_sum
+                    acc[1, :, sl] = value_sum + zero[1, :, sl] * back[64:72]
                 for t in range(CH // 128):
                     lanes = slice(t * 128, t * 128 + 128)
                     base[axis, c * (CH // 128) + t, pl.ds(k8, 8), :] = move[:, lanes]
-                nyqk[2 * axis, pl.ds(k, 1), sl] = back[32:33]
-                nyqk[2 * axis + 1, pl.ds(k, 1), sl] = back[HALF + 32 : HALF + 33]
             acc[0, :, sl] = width_sum
         return carry
 
@@ -423,15 +414,12 @@
     ct, st, a00, a01, a10, a11 = (cols[i] for i in range(6))
     for c in range(G // 128):
         sl = slice(c * 128, (c + 1) * 128)
-        moves, ends = [], []
+        moves = []
         for axis in (0, 1):
             move = base[axis, c, pl.ds(0, NT, stride=8), :]
             for j in range(1, 8):
                 move = move + base[axis, c, pl.ds(j, NT, stride=8), :]
-            nc, ns = nyq[2 * axis, :, sl], nyq[2 * axis + 1, :, sl]
-            kc, ks = nyqk[2 * axis, :, sl], nyqk[2 * axis + 1, :, sl]
-            moves.append(unit * (move + 32.0 * (nc * ks - ns * kc)))
-            ends.append(jnp.sum(nc * kc + ns * ks, axis=0, keepdims=True))
+            moves.append(unit * move)
         mx, my = moves
         r0, r1, r2 = rotated(sl)
         px = ct * r0 + st * r2
@@ -445,8 +433,8 @@
         x, y = ca * x + sa * y, ca * y - sa * x
         x, z = cb * x - sb * z, sb * x + cb * z
         x, y = cc * x + sc * y, cc * y - sc * x
-        curve = jnp.sum(acc[0, :, sl], axis=0, keepdims=True) + 1024.0 * (ends[0] + ends[1])
-        value = jnp.sum(acc[1, :, sl], axis=0, keepdims=True) + ends[1]
+        curve = jnp.sum(acc[0, :, sl], axis=0, keepdims=True)
+        value = jnp.sum(acc[1, :, sl], axis=0, keepdims=True)
         rows = (x, y, z, value / amplitudes[0:1, sl], (-2.0 * blur) * widths[0:1, sl] * curve)
         for i, row in enumerate(rows):
             out[c, 0:1, i * CHUNK : (i + 1) * CHUNK] = row
@@ -474,8 +462,7 @@
             pltpu.VMEM((NT, 128, G), F32),
             pltpu.VMEM((4, G // 128, NT * 8, 128), F32),
             pltpu.VMEM((4, NT, G), F32),
-            pltpu.VMEM((4, NT, G), F32),
-            pltpu.VMEM((4, NT, G), F32),
+            pltpu.VMEM((2, 8, G), F32),
             pltpu.VMEM((2, 32, G), F32),
             pltpu.VMEM((2, 8, G), F32),
             pltpu.VMEM((NT, ROWS, 128), F32),

time: 93 us -> 90.5 us (0.973)
  Pallas kernels: 34.4 us -> 31.9 us
    pallas_call x1, Pallas kernels: 30.2 us -> 27.7 us  [work(): pl.pallas_call(work_kernel, out_shape=jax.ShapeDtypeStruct((SHARES, 1, 6...]
where the time goes in v5:
time: 90.5 us; the launch traced here: 90.1 us
  blocking collectives  54.7 us (60%)
  Pallas kernels  31.9 us (35%)
  between operations  1.97 us (2%)
    all_to_all x3, blocking collectives, swapped(): lax.all_to_all(value, ('tomo', 'tilt'), split_axis=0, concat_axis=0, tile...  36.4 us
    pallas_call x1, Pallas kernels, work(): pl.pallas_call(work_kernel, out_shape=jax.ShapeDtypeStruct((SHARES, 1, 6...  27.7 us
    all_to_all x1, blocking collectives, on_device(): lax.all_to_all(payload, 'tilt', split_axis=0, concat_axis=0, tiled=True)  18.2 us
    pallas_call x1, Pallas kernels, cut(): pl.pallas_call(cut_kernel, out_shape=jax.ShapeDtypeStruct((NP, 40, 128),...  4.19 us

profile of v5, /device:TPU:1, one launch (start us, length us, event | category | flops | bytes accessed | tf_op | source)
XLA Modules:
  0.0 90.1 jit_solution(14798611360837634044)
XLA Ops:
  1.9 4.2 %shard_map.158 = bf16[32,40,128]{2,1,0:T(8,128)(2,1)} custom-call(s32[1,1,2,32]{3,2,1,0:T(2,128)} %bitcast.15, f32[1,1]{1,0:T(1,128)S(6)} %copy.20.angle, f32[1,1]{1,0:T(1,128)S(6)} %copy.21.focus, f32[1,1,6]{2,1,0:T(1,128)} %warp.1, bf16[1,1,1024,1024]{3,2,1,0:T(8,128)(2,1)} %image.1), custom_call_target="tpu_custom_call" | custom-call | tf_op jit(solution)/shard_map/pallas_call | solution.py:141
  6.1 18.2 %all_to_all.20.incoming = bf16[32,40,128]{2,1,0:T(8,128)(2,1)} all-to-all(bf16[32,40,128]{2,1,0:T(8,128)(2,1)} %shard_map.158), channel_id=1, replica_groups=mesh['tomo'=8,'tilt'=32] {'tilt'}, dimensions={0} | all-to-all | bytes 655360 | tf_op jit(solution)/shard_map/all_to_all | solution.py:510
  24.4 27.7 %shard_map.159 = f32[16,1,768]{2,1,0:T(1,128)} custom-call(s32[1]{0:T(128)} %bitcast.1.slot, f32[3,1,32]{2,1,0:T(1,128)} %bitcast.14, bf16[32,40,128]{2,1,0:T(8,128)(2,1)} %all_to_all.20.incoming, f32[3,2048]{1,0:T(4,128)} %centers, f32[1,2048]{1,0:T(1,128)} %bitcast.11, f32[1,2048]{1,0:T(1,128)} %bitcast.12, bf16[128,256]{1,0:T(8,128)(2,1)} %constant.37.clone.right_hi, ...), custom_call_target="tpu_custom_call" | custom-call | tf_op jit(solution)/shard_map/pallas_call | solution.py:456
  52.1 9.9 %all_to_all.21 = f32[16,1,768]{2,1,0:T(1,128)S(1)} all-to-all(f32[16,1,768]{2,1,0:T(1,128)} %shard_map.159), channel_id=1, replica_groups={{0,2,4,6,8,10,12,14,16,18,20,22,24,26,28,30},{1,3,5,7,9,11,13,15,17,19,..., dimensions={0} | all-to-all | bytes 98304 | tf_op jit(solution)/shard_map/all_to_all | solution.py:500
  62.1 17.2 %all_to_all.22 = f32[16,1,768]{2,1,0:T(1,128)S(1)} all-to-all(f32[16,1,768]{2,1,0:T(1,128)S(1)} %broadcast_in_dim.4), channel_id=1, replica_groups={{0,1,32,33,64,65,96,97,128,129,160,161,192,193,224,225},{2,3,34,35,66,6..., dimensions={0} | all-to-all | bytes 98304 | tf_op jit(solution)/shard_map/all_to_all | solution.py:500
  79.4 9.3 %all_to_all.23 = f32[16,1,768]{2,1,0:T(1,128)S(1)} all-to-all(f32[16,1,768]{2,1,0:T(1,128)S(1)} %broadcast_in_dim.5), channel_id=1, replica_groups={{0,2,4,6,8,10,12,14,16,18,20,22,24,26,28,30},{1,3,5,7,9,11,13,15,17,19,..., dimensions={0} | all-to-all | bytes 98304 | tf_op jit(solution)/shard_map/all_to_all | solution.py:500
  88.7 0.1 slice_reduce_fusion
  88.8 0.1 constant_dynamic-slice_fusion
  88.9 0.5 reduce_sum.29
  89.4 0.6 reshape_squeeze.3
  (4 shorter events, 0.1 us)

commit v6 on v5

--- a/solution.py
+++ b/solution.py
@@ -281,7 +281,7 @@
         return spectrum(c, sums)
 
     nought = jnp.zeros((HALF, 128), F32)
-    plus, minus = lax.fori_loop(0, NCH, prepare, (nought, nought), unroll=2)
+    plus, minus = lax.fori_loop(0, NCH, prepare, (nought, nought), unroll=NCH)
     f_plus = aux[1] / (0.25 + (plus + swap(plus)) * (1.0 / NT))
     f_minus = aux[2] / (0.25 + (minus + swap(minus)) * (1.0 / NT))
     radius = aux[0]

time: 90.5 us -> 89 us (0.983)
  Pallas kernels: 31.9 us -> 30.4 us
    pallas_call x1, Pallas kernels: 27.7 us -> 26.3 us  [work(): pl.pallas_call(work_kernel, out_shape=jax.ShapeDtypeStruct((SHARES, 1, 6...]
where the time goes in v6:
time: 89 us; the launch traced here: 88.6 us
  blocking collectives  54.7 us (61%)
  Pallas kernels  30.4 us (34%)
  between operations  1.97 us (2%)
    all_to_all x3, blocking collectives, swapped(): lax.all_to_all(value, ('tomo', 'tilt'), split_axis=0, concat_axis=0, tile...  36.4 us
    pallas_call x1, Pallas kernels, work(): pl.pallas_call(work_kernel, out_shape=jax.ShapeDtypeStruct((SHARES, 1, 6...  26.3 us
    all_to_all x1, blocking collectives, on_device(): lax.all_to_all(payload, 'tilt', split_axis=0, concat_axis=0, tiled=True)  18.2 us
    pallas_call x1, Pallas kernels, cut(): pl.pallas_call(cut_kernel, out_shape=jax.ShapeDtypeStruct((NP, 40, 128),...  4.19 us

profile of v6, /device:TPU:1, one launch (start us, length us, event | category | flops | bytes accessed | tf_op | source)
XLA Modules:
  0.0 88.6 jit_solution(6184600844546581257)
XLA Ops:
  1.9 4.2 %shard_map.158 = bf16[32,40,128]{2,1,0:T(8,128)(2,1)} custom-call(s32[1,1,2,32]{3,2,1,0:T(2,128)} %bitcast.15, f32[1,1]{1,0:T(1,128)S(6)} %copy.20.angle, f32[1,1]{1,0:T(1,128)S(6)} %copy.21.focus, f32[1,1,6]{2,1,0:T(1,128)} %warp.1, bf16[1,1,1024,1024]{3,2,1,0:T(8,128)(2,1)} %image.1), custom_call_target="tpu_custom_call" | custom-call | tf_op jit(solution)/shard_map/pallas_call | solution.py:141
  6.1 18.2 %all_to_all.20.incoming = bf16[32,40,128]{2,1,0:T(8,128)(2,1)} all-to-all(bf16[32,40,128]{2,1,0:T(8,128)(2,1)} %shard_map.158), channel_id=1, replica_groups=mesh['tomo'=8,'tilt'=32] {'tilt'}, dimensions={0} | all-to-all | bytes 655360 | tf_op jit(solution)/shard_map/all_to_all | solution.py:510
  24.4 26.3 %shard_map.159 = f32[16,1,768]{2,1,0:T(1,128)} custom-call(s32[1]{0:T(128)} %bitcast.1.slot, f32[3,1,32]{2,1,0:T(1,128)} %bitcast.14, bf16[32,40,128]{2,1,0:T(8,128)(2,1)} %all_to_all.20.incoming, f32[3,2048]{1,0:T(4,128)} %centers, f32[1,2048]{1,0:T(1,128)} %bitcast.11, f32[1,2048]{1,0:T(1,128)} %bitcast.12, bf16[128,256]{1,0:T(8,128)(2,1)} %constant.37.clone.right_hi, ...), custom_call_target="tpu_custom_call" | custom-call | tf_op jit(solution)/shard_map/pallas_call | solution.py:456
  50.6 9.9 %all_to_all.21 = f32[16,1,768]{2,1,0:T(1,128)S(1)} all-to-all(f32[16,1,768]{2,1,0:T(1,128)} %shard_map.159), channel_id=1, replica_groups={{0,2,4,6,8,10,12,14,16,18,20,22,24,26,28,30},{1,3,5,7,9,11,13,15,17,19,..., dimensions={0} | all-to-all | bytes 98304 | tf_op jit(solution)/shard_map/all_to_all | solution.py:500
  60.6 17.2 %all_to_all.22 = f32[16,1,768]{2,1,0:T(1,128)S(1)} all-to-all(f32[16,1,768]{2,1,0:T(1,128)S(1)} %broadcast_in_dim.4), channel_id=1, replica_groups={{0,1,32,33,64,65,96,97,128,129,160,161,192,193,224,225},{2,3,34,35,66,6..., dimensions={0} | all-to-all | bytes 98304 | tf_op jit(solution)/shard_map/all_to_all | solution.py:500
  77.9 9.3 %all_to_all.23 = f32[16,1,768]{2,1,0:T(1,128)S(1)} all-to-all(f32[16,1,768]{2,1,0:T(1,128)S(1)} %broadcast_in_dim.5), channel_id=1, replica_groups={{0,2,4,6,8,10,12,14,16,18,20,22,24,26,28,30},{1,3,5,7,9,11,13,15,17,19,..., dimensions={0} | all-to-all | bytes 98304 | tf_op jit(solution)/shard_map/all_to_all | solution.py:500
  87.2 0.1 slice_reduce_fusion
  87.3 0.1 constant_dynamic-slice_fusion
  87.4 0.5 reduce_sum.29
  88.0 0.6 reshape_squeeze.3
  (4 shorter events, 0.1 us)
